TPU v7x, 32 devices: a whole 2x2x4 slice. The times are simulated.
32 devices in a mesh: wrap: 8 (over y, x, core), normal: 4 (over z).
Axes of the slice: x: 2, y: 2, z: 4, core: 2. Of those that a mesh axis runs over, the one named last changes fastest.
Arguments:
- residual: float32 [5, 2, 256, 1024], P(None, None, 'normal', 'wrap'), may hold values from -144 to 144
- courant_xi: float32 [5, 2, 256, 1024], P(None, None, 'normal', 'wrap'), may hold values from -300 to 300
- courant_eta: float32 [5, 2, 256, 1024], P(None, None, 'normal', 'wrap'), may hold values from -300 to 300
- dissip_xi: float32 [2, 256, 1024], P(None, 'normal', 'wrap'), may hold values from 0.02 to 2
- dissip_eta: float32 [2, 256, 1024], P(None, 'normal', 'wrap'), may hold values from 0.02 to 2
- coupling: bfloat16 [5, 5, 2, 256, 1024], P(None, None, None, 'normal', 'wrap'), may hold values from -2.5 to 2.5
Outputs:
- update: float32 [5, 2, 256, 1024], P(None, None, 'normal', 'wrap')
All inputs are finite; a program needn't handle non-finite values.
Results may differ from a plain program's by a relative error of at most 0.0003.
Values sent between devices are 32-bit elements; how exact they have to be, the bound alone decides.
No kernel may reach another device: no remote copies, remote signals or barrier semaphores. Data moves between devices by JAX's collectives and lax.ppermute only.
A program may use at most 128 MiB of HBM per device.

v0:
```python
import functools

import jax
import jax.numpy as jnp
from jax import lax
from jax.experimental import pallas as pl
from jax.experimental.pallas import tpu as pltpu
from jax.sharding import PartitionSpec as P

MATRIX = 16
SOURCE = 4
VALUES = MATRIX + SOURCE
UP = 8
CHUNK_DOWN = 9
MERGE_DOWN = 12
CHUNKS = 8


def inverse(a, b, c, d):
    scale = 1.0 / (a * d - b * c)
    return (d * scale, -b * scale, -c * scale, a * scale)


def times(x, y):
    return (
        x[0] * y[0] + x[1] * y[2],
        x[0] * y[1] + x[1] * y[3],
        x[2] * y[0] + x[3] * y[2],
        x[2] * y[1] + x[3] * y[3],
    )


def apply(x, v):
    return (x[0] * v[0] + x[1] * v[1], x[2] * v[0] + x[3] * v[1])


def minus(x, y):
    return tuple(a - b for a, b in zip(x, y))


def plus(x, y):
    return tuple(a + b for a, b in zip(x, y))


def negative(x):
    return tuple(-a for a in x)


def quads(element):
    return (element[0:4], element[4:8], element[8:12], element[12:16])


def merge_matrix(first, second):
    ll, lm, ml, mm = quads(first)
    nn, mr, rm, rr = quads(second)
    pivot = inverse(*plus(mm, nn))
    wl = times(pivot, ml)
    wr = times(pivot, mr)
    merged = (
        minus(ll, times(lm, wl))
        + negative(times(lm, wr))
        + negative(times(rm, wl))
        + minus(rr, times(rm, wr))
    )
    return merged, wl + wr, pivot + lm + rm


def merge_source(down, first, second):
    pivot, lm, rm = down[0:4], down[4:8], down[8:12]
    w = apply(pivot, plus(first[2:4], second[0:2]))
    return minus(first[0:2], apply(lm, w)) + minus(second[2:4], apply(rm, w)), w


def merge(first, second):
    matrix, up, down = merge_matrix(first[:MATRIX], second[:MATRIX])
    source, w = merge_source(down, first[MATRIX:], second[MATRIX:])
    return matrix + source, up, w


def inner(up, w, left, right):
    return minus(minus(w, apply(up[0:4], left)), apply(up[4:8], right))


def chunk_matrix(speed, damp, cells):
    def link(i):
        p = 2.0 * (damp(i) + damp(i + 1))
        q = 0.25 * (speed(i) + speed(i + 1))
        return q - p, -q - p

    def centre(i):
        return 1.0 + damp(i - 1) + 4.0 * damp(i) + damp(i + 1)

    b0, b1 = damp(0), damp(1)
    quarter = 0.25 * speed(0)
    up, low = link(0)
    zero = jnp.zeros_like(b0)
    ll = (b0, quarter - 2.0 * b0, -quarter - 2.0 * b0, 1.0 + 4.0 * b0 + b1)
    lk = (b0, zero, up, b1)
    kl = (b0, low, zero, b1)
    up, low = link(1)
    kk = (centre(1), up, low, centre(2))
    pairs = (cells - 2) // 2
    for k in range(1, pairs + 1):
        i = 2 * k
        pivot = inverse(*kk)
        wl = times(pivot, kl)
        up, low = link(i)
        here, there = damp(i), damp(i + 1)
        wr = (
            pivot[0] * here + pivot[1] * up,
            pivot[1] * there,
            pivot[2] * here + pivot[3] * up,
            pivot[3] * there,
        )
        yield wl + wr, pivot + lk + (low,), (here, there)

        def below(x):
            return (
                here * x[0] + low * x[2],
                here * x[1] + low * x[3],
                there * x[2],
                there * x[3],
            )

        ll = minus(ll, times(lk, wl))
        lk = negative(times(lk, wr))
        kl = negative(below(wl))
        if k < pairs:
            up, low_next = link(i + 1)
            kk = (centre(i + 1), up, low_next, centre(i + 2))
        else:
            quarter = 0.25 * speed(i + 1)
            kk = (
                1.0 + here + 4.0 * there,
                quarter - 2.0 * there,
                -quarter - 2.0 * there,
                there,
            )
        kk = minus(kk, below(wr))
    yield ll + lk + kl + kk


def pair_source(down, damps, left, pair, following):
    pivot, lk, low = down[0:4], down[4:8], down[8]
    w = apply(pivot, pair)
    left = minus(left, apply(lk, w))
    following = minus(following, (damps[0] * w[0] + low * w[1], damps[1] * w[1]))
    return left, following, w


def pair_of(source, k, cells):
    if k == (cells - 2) // 2:
        last = source(cells - 1)
        return (last, jnp.zeros_like(last))
    return (source(2 * k + 1), source(2 * k + 2))


def first_pair(source):
    first = source(0)
    return (jnp.zeros_like(first), first)


def blocks(rows, size):
    return [(at, min(size, rows - at)) for at in range(0, rows, size)]


def get(ref, count, at, size, base=0):
    return tuple(ref[base + v, pl.ds(at, size), :] for v in range(count))


def put(ref, values, at, size, base=0):
    for v, value in enumerate(values):
        ref[base + v, pl.ds(at, size), :] = value


def get_both(ref, count, at, size):
    return tuple(
        tuple(ref[v, pl.ds(2 * at + half, size, stride=2), :] for v in range(count))
        for half in (0, 1)
    )


def levels_of(lines):
    sizes = []
    rows = lines * CHUNKS
    while rows > lines:
        rows //= 2
        sizes.append(rows)
    return sizes


def split_all(top_ref, end_refs, up_refs, w_refs, sizes):
    source = top_ref
    for rows, target, ups, ws in zip(
        reversed(sizes), end_refs, reversed(up_refs), reversed(w_refs)
    ):
        for at, size in blocks(rows, 8):
            ends = get(source, 4, at, size)
            left, right = ends[0:2], ends[2:4]
            middle = inner(get(ups, UP, at, size), get(ws, 2, at, size), left, right)
            for v in range(2):
                target[v, pl.ds(2 * at, size, stride=2), :] = left[v]
                target[v, pl.ds(2 * at + 1, size, stride=2), :] = middle[v]
                target[2 + v, pl.ds(2 * at, size, stride=2), :] = middle[v]
                target[2 + v, pl.ds(2 * at + 1, size, stride=2), :] = right[v]
        source = target
    return source


def back_substitute(ends_ref, up_ref, w_ref, cells, at, size, store):
    ends = get(ends_ref, 4, at, size)
    left, following = ends[0:2], ends[2:4]
    store(0, left[1])
    store(cells - 1, following[0])
    for k in range((cells - 2) // 2 - 1, -1, -1):
        following = inner(
            get(up_ref, UP, at, size, k * UP), get(w_ref, 2, at, size, k * 2), left, following
        )
        store(2 * k + 1, following[0])
        store(2 * k + 2, following[1])


def close_ring(own, rest):
    ll, lr, rl, rr = quads(own)
    nn, nm, mn, mm = quads(rest)
    b = plus(lr, mn)
    c = plus(rl, nm)
    pivot = inverse(*plus(rr, nn))
    f = plus(own[16:18], rest[18:20])
    g = plus(own[18:20], rest[16:18])
    bd = times(b, pivot)
    left = apply(inverse(*minus(plus(ll, mm), times(bd, c))), minus(f, apply(bd, g)))
    right = apply(pivot, minus(g, apply(c, left)))
    return left, right


def open_ends(axis):
    place = lax.axis_index(axis)
    last = lax.axis_size(axis) - 1
    return jnp.where(place > 0, 1.0, 0.0), jnp.where(place < last, 1.0, 0.0)


def is_second(axis, bit):
    return lax.rem(lax.axis_index(axis) // (1 << bit), 2) == 1


def choose(second, one, other):
    return tuple(jnp.where(second, a, b) for a, b in zip(one, other))


def flat(ref, count, rows, at, size):
    return tuple(ref[pl.ds(v * rows + at, size), :] for v in range(count))


def put_flat(ref, values, rows, at, size):
    for v, value in enumerate(values):
        ref[pl.ds(v * rows + at, size), :] = value


def round_down(ups, ws, axis, bits, at, size, left, right):
    for bit in reversed(range(bits)):
        middle = inner(get(ups[bit], UP, at, size), get(ws[bit], 2, at, size), left, right)
        second = is_second(axis, bit)
        left, right = choose(second, middle, left), choose(second, right, middle)
    return left, right


def copies(pairs, sems, first=0):
    started = []
    for i, (source, target) in enumerate(pairs):
        copy = pltpu.make_async_copy(source, target, sems.at[first + i])
        copy.start()
        started.append(copy)
    return started


def wrap_down(fields, cells, *refs):
    residual, courant, dissip, wall_courant, wall_dissip = refs[0:5]
    packed, chunk_up, chunk_w = refs[5:8]
    ups, ws = refs[8:11], refs[11:14]
    wall_speed, wall_damp = refs[14:16]
    source_in, speed_in, damp_in, source_t, speed_t, damp_t = refs[16:22]
    elements, sems = refs[22:26], refs[26]
    lanes = damp_in.shape[0]
    length = cells * CHUNKS
    parts = [(0, 2), (2, fields)] if fields > 2 else [(0, fields)]
    moves = [(dissip, damp_in)]
    for first, last in parts:
        rows = pl.ds(first * lanes, (last - first) * lanes)
        moves.append((courant.at[rows], speed_in.at[rows]))
        moves.append((residual.at[rows], source_in.at[rows]))
    started = copies(moves, sems)
    started[0].wait()
    damp_t[...] = damp_in[...].T
    for part, (first, last) in enumerate(parts):
        at, size, repeat = first * CHUNKS, (last - first) * CHUNKS, last - first
        for inner_copy, taken, turned in (
            (started[1 + 2 * part], speed_in, speed_t),
            (started[2 + 2 * part], source_in, source_t),
        ):
            inner_copy.wait()
            for field in range(first, last):
                turned[pl.ds(field * length, length), :] = taken[pl.ds(field * lanes, lanes), :].T

        if part == 0:
            moves = [(wall_dissip, wall_damp), (wall_courant, wall_speed)]
            wall_started = copies(moves, sems, len(started))

        def speed(i):
            return speed_t[pl.ds(at * cells + i, size, stride=cells), :]

        def source(i):
            return source_t[pl.ds(at * cells + i, size, stride=cells), :]

        def damp(i):
            rows = damp_t[pl.ds(i, CHUNKS, stride=cells), :]
            return jnp.concatenate([rows] * repeat, axis=0) if repeat > 1 else rows

        left, pair = first_pair(source), pair_of(source, 0, cells)
        for k, step in enumerate(chunk_matrix(speed, damp, cells)):
            if k == (cells - 2) // 2:
                put(elements[0], step + left + pair, at, size)
                break
            up, down, damps = step
            left, pair, w = pair_source(down, damps, left, pair, pair_of(source, k + 1, cells))
            put(chunk_up, up, at, size, k * UP)
            put(chunk_w, w, at, size, k * 2)
    for level, rows in enumerate(levels_of(fields)):
        for at, size in blocks(rows, 8):
            merged, up, w = merge(*get_both(elements[level], VALUES, at, size))
            put(elements[level + 1], merged, at, size)
            put(ups[level], up, at, size)
            put(ws[level], w, at, size)
    for v in range(VALUES):
        packed[pl.ds(v * fields, fields), :] = elements[-1][v]
    for copy in wall_started:
        copy.wait()


def wrap_round(fields, bit, own, other, after, packed, up_out, w_out):
    second = is_second("wrap", bit)
    for at, size in blocks(fields, 8):
        mine = flat(own, VALUES, fields, at, size)
        theirs = flat(other, VALUES, fields, at, size)
        merged, up, w = merge(choose(second, theirs, mine), choose(second, mine, theirs))
        put_flat(packed, merged, fields, at, size)
        put(up_out, up, at, size)
        put(w_out, w, at, size)


def wall_matrix(fields, span, cells, *refs):
    speed_in, damp_in = refs[0:2]
    packed, damp_out, chunk_up, chunk_down = refs[2:6]
    ups, downs = refs[6:9], refs[9:12]
    elements = refs[12:16]
    size = span * CHUNKS
    for field in range(fields):
        at = field * size

        def speed(i):
            return speed_in[pl.ds(at * cells + i, size, stride=cells), :]

        def damp(i):
            return damp_in[pl.ds(i, size, stride=cells), :]

        for k, step in enumerate(chunk_matrix(speed, damp, cells)):
            if k == (cells - 2) // 2:
                put(elements[0], step, at, size)
                break
            up, down, damps = step
            put(chunk_up, up, at, size, k * UP)
            put(chunk_down, down, at, size, k * CHUNK_DOWN)
            if field == 0:
                put(damp_out, damps, 0, size, k * 2)
    lines = fields * span
    for level, rows in enumerate(levels_of(lines)):
        for at, size in blocks(rows, 8):
            merged, up, down = merge_matrix(*get_both(elements[level], MATRIX, at, size))
            put(elements[level + 1], merged, at, size)
            put(ups[level], up, at, size)
            put(downs[level], down, at, size)
    not_first, not_last = open_ends("normal")
    for v in range(MATRIX):
        value = elements[-1][v]
        if v in (0, 1, 2, 4, 5, 8, 10):
            value = value * not_first
        if v in (5, 7, 10, 11, 13, 14, 15):
            value = value * not_last
        packed[pl.ds(v * lines, lines), :] = value


def wall_round(lines, bit, final, own, other, *refs):
    started = []
    if final:
        coupling, packed, up_out, down_out, outer_out, coupling_out, sems = refs
        count = sems.shape[0]
        parts = [pl.ds(k * count, count) for k in range(count)]
        started = copies([(coupling.at[k], coupling_out.at[k]) for k in parts], sems)
    else:
        packed, up_out, down_out = refs
    second = is_second("normal", bit)
    upper = is_second("normal", bit + 1)
    for at, size in blocks(lines, 8):
        mine = flat(own, MATRIX, lines, at, size)
        theirs = flat(other, MATRIX, lines, at, size)
        merged, up, down = merge_matrix(
            choose(second, theirs, mine), choose(second, mine, theirs)
        )
        put(up_out, up, at, size)
        put(down_out, down, at, size)
        if not final:
            put_flat(packed, merged, lines, at, size)
            continue
        ll, lr, rl, rr = quads(merged)
        outer, into = choose(upper, rr, ll), choose(upper, rl, lr)
        out, middle = choose(upper, lr, rl), choose(upper, ll, rr)
        is_upper = jnp.where(upper, 1.0, 0.0)
        pivot = inverse(
            outer[0] + (1.0 - is_upper), outer[1], outer[2], outer[3] + is_upper
        )
        put_flat(packed, minus(middle, times(out, times(pivot, into))), lines, at, size)
        put(outer_out, pivot + into + out, at, size)
    for copy in started:
        copy.wait()


def wall_source_round(lines, bit, own, other, down_in, packed, w_out):
    second = is_second("normal", bit)
    for at, size in blocks(lines, 8):
        mine = flat(own, SOURCE, lines, at, size)
        theirs = flat(other, SOURCE, lines, at, size)
        merged, w = merge_source(
            get(down_in, MERGE_DOWN, at, size),
            choose(second, theirs, mine),
            choose(second, mine, theirs),
        )
        put_flat(packed, merged, lines, at, size)
        put(w_out, w, at, size)


def reduce_source(down, factors, second, upper, mine, theirs):
    merged, w = merge_source(
        down, choose(second, theirs, mine), choose(second, mine, theirs)
    )
    outer = apply(factors[0:4], choose(upper, merged[2:4], merged[0:2]))
    centre = choose(upper, merged[0:2], merged[2:4])
    return minus(centre, apply(factors[8:12], outer)), outer, w


def wall_share(lines, bit, own, down_in, outer_in, matrix, share, bundle, copy):
    share[pl.ds(2 * lines, 2 * lines), :] = jnp.zeros((2 * lines, share.shape[1]), jnp.float32)
    copy[...] = own[...]
    bundle[pl.ds(2 * lines, 4 * lines), :] = matrix[...]
    second, upper = is_second("normal", bit), is_second("normal", bit + 1)
    for at, size in blocks(lines, 8):
        mine = flat(own, SOURCE, lines, at, size)
        none = tuple(jnp.zeros_like(value) for value in mine)
        down, factors = get(down_in, MERGE_DOWN, at, size), get(outer_in, 12, at, size)
        part, _, _ = reduce_source(down, factors, second, upper, mine, none)
        put_flat(share, part, lines, at, size)
        put_flat(bundle, part, lines, at, size)


def wrap_three(fields, own, following, before, packed, back_up, back_w, next_up, next_w):
    for at, size in blocks(fields, 8):
        run, up, w = merge(
            flat(before, VALUES, fields, at, size), flat(own, VALUES, fields, at, size)
        )
        put(back_up, up, at, size)
        put(back_w, w, at, size)
        run, up, w = merge(run, flat(following, VALUES, fields, at, size))
        put(next_up, up, at, size)
        put(next_w, w, at, size)
        put_flat(packed, run, fields, at, size)


def middle(fields, span, wrap_cells, wall_cells, bits, *refs):
    three, opposite, back_up, back_w, next_up, next_w = refs[0:6]
    refs = refs[6:]
    round_ups, round_ws, refs = refs[:bits], refs[bits : 2 * bits], refs[2 * bits :]
    chunk_up, chunk_w, ups, ws = refs[0], refs[1], refs[2:5], refs[5:8]
    coupling, damps_in, chunk_down, downs = refs[8], refs[9], refs[10], refs[11:14]
    packed, wall_w, wall_ws = refs[14], refs[15], refs[16:19]
    ends, solved_t, solved, mixed = refs[19:23], refs[23], refs[24], refs[25]
    sources = refs[26:30]

    for at, size in blocks(fields, 8):
        outer_left, outer_right = close_ring(
            flat(three, VALUES, fields, at, size), flat(opposite, VALUES, fields, at, size)
        )
        right = inner(get(next_up, UP, at, size), get(next_w, 2, at, size), outer_left, outer_right)
        left = inner(get(back_up, UP, at, size), get(back_w, 2, at, size), outer_left, right)
        left, right = round_down(round_ups, round_ws, "wrap", bits, at, size, left, right)
        put(ends[0], left + right, at, size)
    last = split_all(ends[0], ends[1:], ups, ws, levels_of(fields))
    length = wrap_cells * CHUNKS
    for at, size in blocks(fields * CHUNKS, 16):

        def store(i, value):
            solved_t[pl.ds(at * wrap_cells + i, size, stride=wrap_cells), :] = value

        back_substitute(last, chunk_up, chunk_w, wrap_cells, at, size, store)
    lanes = solved.shape[0] // fields
    for field in range(fields):
        solved[pl.ds(field * lanes, lanes), :] = solved_t[pl.ds(field * length, length), :].T

    for at, size in blocks(lanes, 16):
        update = [solved[pl.ds(j * lanes + at, size), :] for j in range(fields)]
        for k in range(fields):
            total = coupling[k * fields, pl.ds(at, size), :].astype(jnp.float32) * update[0]
            for j in range(1, fields):
                factor = coupling[k * fields + j, pl.ds(at, size), :]
                total = total + factor.astype(jnp.float32) * update[j]
            mixed[pl.ds(k * lanes + at, size), :] = total

    pairs = (wall_cells - 2) // 2
    size = span * CHUNKS
    for field in range(fields):
        at = field * size

        def source(i):
            return mixed[pl.ds(at * wall_cells + i, size, stride=wall_cells), :]

        left, pair = first_pair(source), pair_of(source, 0, wall_cells)
        for k in range(pairs):
            left, pair, w = pair_source(
                get(chunk_down, CHUNK_DOWN, at, size, k * CHUNK_DOWN),
                get(damps_in, 2, 0, size, k * 2),
                left,
                pair,
                pair_of(source, k + 1, wall_cells),
            )
            put(wall_w, w, at, size, k * 2)
        put(sources[0], left + pair, at, size)
    lines = fields * span
    for level, rows in enumerate(levels_of(lines)):
        for at, size in blocks(rows, 8):
            down = get(downs[level], MERGE_DOWN, at, size)
            merged, w = merge_source(down, *get_both(sources[level], SOURCE, at, size))
            put(sources[level + 1], merged, at, size)
            put(wall_ws[level], w, at, size)
    not_first, not_last = open_ends("normal")
    for v, keep in enumerate((not_first, None, None, not_last)):
        value = sources[-1][v]
        packed[pl.ds(v * lines, lines), :] = value if keep is None else value * keep


def wall_up(fields, span, cells, bits, *refs):
    own_matrix, down_in, outer_in, own, bundle, other, share = refs[0:7]
    refs = refs[7:]
    round_ups, round_ws, refs = refs[: bits + 1], refs[bits + 1 : 2 * bits + 1], refs[2 * bits + 1 :]
    chunk_up, chunk_w, ups, ws = refs[0], refs[1], refs[2:5], refs[5:8]
    update = refs[8]
    ends, result, sems = refs[9:13], refs[13], refs[14]
    lines = fields * span
    second, upper = is_second("normal", bits), is_second("normal", bits + 1)
    for at, size in blocks(lines, 8):
        down, factors = get(down_in, MERGE_DOWN, at, size), get(outer_in, 12, at, size)
        part, outer, w = reduce_source(
            down,
            factors,
            second,
            upper,
            flat(own, SOURCE, lines, at, size),
            flat(other, SOURCE, lines, at, size),
        )
        opposite = flat(bundle, 6, lines, at, size)
        shares = plus(opposite[0:2], flat(share, 2, lines, at, size))
        matrix = plus(flat(own_matrix, 4, lines, at, size), opposite[2:6])
        centre = apply(inverse(*matrix), plus(part, shares))
        outer = minus(outer, apply(factors[0:4], apply(factors[4:8], centre)))
        left, right = choose(upper, centre, outer), choose(upper, outer, centre)
        between = inner(get(round_ups[bits], UP, at, size), w, left, right)
        left, right = choose(second, between, left), choose(second, right, between)
        left, right = round_down(round_ups, round_ws, "normal", bits, at, size, left, right)
        put(ends[0], left + right, at, size)
    last = split_all(ends[0], ends[1:], ups, ws, levels_of(lines))
    size = span * CHUNKS
    length = size * cells
    started = []
    for field in range(fields):
        at = field * size

        def store(i, value):
            result[pl.ds(at * cells + i, size, stride=cells), :] = value

        back_substitute(last, chunk_up, chunk_w, cells, at, size, store)
        rows = pl.ds(field * length, length)
        copy = pltpu.make_async_copy(result.at[rows], update.at[rows], sems.at[field])
        copy.start()
        started.append(copy)
    for copy in started:
        copy.wait()


def f32(*shape):
    return jax.ShapeDtypeStruct(shape, jnp.float32)


def vmem(*shape):
    return pltpu.VMEM(shape, jnp.float32)


IN_VMEM = pl.BlockSpec(memory_space=pltpu.VMEM)
IN_HBM = pl.BlockSpec(memory_space=pltpu.HBM)
PARAMS = pltpu.CompilerParams(vmem_limit_bytes=24 * 2**20)


def kernel(name, body, ins, outs, scratch, flops):
    in_bytes = sum(a.size * a.dtype.itemsize for a, _ in ins)
    out_bytes = sum(a.size * 4 for a, _ in outs)
    outputs = pl.pallas_call(
        body,
        out_shape=[a for a, _ in outs],
        in_specs=[spec for _, spec in ins],
        out_specs=[spec for _, spec in outs],
        scratch_shapes=scratch,
        compiler_params=PARAMS,
        cost_estimate=pl.CostEstimate(
            flops=flops, bytes_accessed=in_bytes + out_bytes, transcendentals=0
        ),
        name=name,
    )(*[a for a, _ in ins])
    return list(outputs)


def inside(arrays):
    return [(a, IN_VMEM) for a in arrays]


def outside(arrays):
    return [(pltpu.with_memory_space_constraint(a, pltpu.HBM), IN_HBM) for a in arrays]


def exchange(array, axis, mask):
    count = lax.axis_size(axis)
    return lax.ppermute(array, axis, [(i, i ^ mask) for i in range(count)])


def pass_on(array, axis, bit, targets, swap=0):
    count = lax.axis_size(axis)

    def target(i):
        place = i // (1 << bit) % 4
        return (i + (targets[place] - place) * (1 << bit)) ^ swap

    return lax.ppermute(array, axis, [(i, target(i)) for i in range(count)])


def local(residual, courant_xi, courant_eta, dissip_xi, dissip_eta, coupling):
    fields, span, high, wide = residual.shape
    lanes = span * high
    wrap_cells, wall_cells = wide // CHUNKS, high // CHUNKS
    wrap_pairs, wall_pairs = (wrap_cells - 2) // 2, (wall_cells - 2) // 2
    wrap_count, wall_count = lax.axis_size("wrap"), lax.axis_size("normal")
    lines = fields * span
    wrap_levels, wall_levels = levels_of(fields), levels_of(lines)
    wrap_rows, wall_rows = fields * CHUNKS, lines * CHUNKS

    def rows_of(array):
        return array.reshape(-1, wide)

    wrap_bits = wrap_count.bit_length() - 3
    wall_bits = wall_count.bit_length() - 3
    results = kernel(
        "wrap_down",
        functools.partial(wrap_down, fields, wrap_cells),
        outside(
            [rows_of(a) for a in (residual, courant_xi, dissip_xi, courant_eta, dissip_eta)]
        ),
        inside(
            [
                f32(VALUES * fields, lanes),
                f32(wrap_pairs * UP, wrap_rows, lanes),
                f32(wrap_pairs * 2, wrap_rows, lanes),
            ]
            + [f32(UP, n, lanes) for n in wrap_levels]
            + [f32(2, n, lanes) for n in wrap_levels]
            + [f32(fields * lanes, wide), f32(lanes, wide)]
        ),
        [vmem(fields * lanes, wide)] * 2
        + [vmem(lanes, wide)]
        + [vmem(fields * wide, lanes)] * 2
        + [vmem(wide, lanes)]
        + [vmem(VALUES, n, lanes) for n in [wrap_rows] + wrap_levels]
        + [pltpu.SemaphoreType.DMA((7,))],
        100 * residual.size,
    )
    element, wrap_factors, wall_inputs = results[0], results[1:9], results[9:11]
    results = kernel(
        "wall_matrix",
        functools.partial(wall_matrix, fields, span, wall_cells),
        inside(wall_inputs),
        inside(
            [
                f32(MATRIX * lines, wide),
                f32(wall_pairs * 2, span * CHUNKS, wide),
                f32(wall_pairs * UP, wall_rows, wide),
                f32(wall_pairs * CHUNK_DOWN, wall_rows, wide),
            ]
            + [f32(UP, n, wide) for n in wall_levels]
            + [f32(MERGE_DOWN, n, wide) for n in wall_levels]
        ),
        [vmem(MATRIX, n, wide) for n in [wall_rows] + wall_levels],
        100 * residual.size,
    )
    matrix, damps, chunk_up, chunk_down = results[0:4]
    wall_ups, wall_downs = results[4:7], results[7:10]
    wrap_ups, wrap_ws = [], []
    for bit in range(wrap_bits):
        element, up, w = kernel(
            f"wrap_round_{bit}",
            functools.partial(wrap_round, fields, bit),
            inside([element, exchange(element, "wrap", 1 << bit), damps]),
            inside([f32(VALUES * fields, lanes), f32(UP, fields, lanes), f32(2, fields, lanes)]),
            [],
            200 * fields * lanes,
        )
        wrap_ups.append(up)
        wrap_ws.append(w)
    swap = 1 if wrap_bits > 0 else 0
    before, following, opposite = (
        pass_on(element, "wrap", wrap_bits, targets, swap)
        for targets in ((1, 2, 3, 0), (3, 0, 1, 2), (2, 3, 0, 1))
    )
    three = kernel(
        "wrap_three",
        functools.partial(wrap_three, fields),
        inside([element, following, before]),
        inside(
            [f32(VALUES * fields, lanes)]
            + [f32(UP, fields, lanes), f32(2, fields, lanes)] * 2
        ),
        [],
        400 * fields * lanes,
    )
    round_ups, round_downs = [], []
    for bit in range(wall_bits + 1):
        final = bit == wall_bits
        matrix, up, down, *extra = kernel(
            f"wall_round_{bit}",
            functools.partial(wall_round, lines, bit, final),
            inside([matrix, exchange(matrix, "normal", 1 << bit)])
            + (outside([coupling.reshape(fields * fields, lanes, wide)]) if final else []),
            inside(
                [
                    f32((4 if final else MATRIX) * lines, wide),
                    f32(UP, lines, wide),
                    f32(MERGE_DOWN, lines, wide),
                ]
                + (
                    [
                        f32(12, lines, wide),
                        jax.ShapeDtypeStruct((fields * fields, lanes, wide), coupling.dtype),
                    ]
                    if final
                    else []
                )
            ),
            [pltpu.SemaphoreType.DMA((fields,))] if final else [],
            200 * lines * wide,
        )
        round_ups.append(up)
        round_downs.append(down)
    outer, coupling_in = extra[:1], extra[1]
    source, *wall_ws = kernel(
        "middle",
        functools.partial(middle, fields, span, wrap_cells, wall_cells, wrap_bits),
        inside(
            [three[0], opposite]
            + three[1:]
            + wrap_ups
            + wrap_ws
            + wrap_factors
            + [coupling_in, damps, chunk_down]
            + wall_downs
        ),
        inside(
            [f32(SOURCE * lines, wide), f32(wall_pairs * 2, wall_rows, wide)]
            + [f32(2, n, wide) for n in wall_levels]
        ),
        [vmem(4, n, lanes) for n in reversed([wrap_rows] + wrap_levels)]
        + [vmem(fields * wide, lanes), vmem(fields * lanes, wide), vmem(fields * lanes, wide)]
        + [vmem(SOURCE, n, wide) for n in [wall_rows] + wall_levels],
        100 * residual.size,
    )
    round_ws = []
    for bit in range(wall_bits):
        source, w = kernel(
            f"wall_source_round_{bit}",
            functools.partial(wall_source_round, lines, bit),
            inside([source, exchange(source, "normal", 1 << bit), round_downs[bit]]),
            inside([f32(SOURCE * lines, wide), f32(2, lines, wide)]),
            [],
            50 * lines * wide,
        )
        round_ws.append(w)
    share, bundle, source = kernel(
        "wall_share",
        functools.partial(wall_share, lines, wall_bits),
        inside([source, round_downs[wall_bits]] + outer + [matrix]),
        inside([f32(SOURCE * lines, wide), f32(6 * lines, wide), f32(SOURCE * lines, wide)]),
        [],
        50 * lines * wide,
    )
    (update,) = kernel(
        "wall_up",
        functools.partial(wall_up, fields, span, wall_cells, wall_bits),
        inside(
            [matrix, round_downs[wall_bits]]
            + outer
            + [
                source,
                pass_on(bundle, "normal", wall_bits, (2, 3, 1, 0)),
                exchange(source, "normal", 1 << wall_bits),
                pass_on(share, "normal", wall_bits, (3, 2, 0, 1)),
            ]
            + round_ups
            + round_ws
            + [chunk_up, wall_ws[0]]
            + wall_ups
            + wall_ws[1:]
        ),
        [(f32(fields * lanes, wide), IN_HBM)],
        [vmem(4, n, wide) for n in reversed([wall_rows] + wall_levels)]
        + [vmem(fields * lanes, wide), pltpu.SemaphoreType.DMA((fields,))],
        30 * residual.size,
    )
    return update.reshape(residual.shape)


def solution(mesh):
    placed = (
        P(None, None, "normal", "wrap"),
        P(None, None, "normal", "wrap"),
        P(None, None, "normal", "wrap"),
        P(None, "normal", "wrap"),
        P(None, "normal", "wrap"),
        P(None, None, None, "normal", "wrap"),
    )
    return jax.shard_map(
        local,
        mesh=mesh,
        in_specs=placed,
        out_specs=P(None, None, "normal", "wrap"),
        check_vma=False,
    )
```

profile of v0, /device:TPU:0, one launch (start us, length us, event | category | flops | bytes accessed | tf_op | source)
XLA Modules:
  0.0 21.9 jit_solution(4126817316871707693)
XLA Ops:
  0.0 2.2 %wrap_down.1 = (f32[100,128]{1,0:T(8,128)S(1)}, f32[56,40,128]{2,1,0:T(8,128)S(1)}, f32[14,40,128]{2,1,0:T(8,128)S(1)}, f32[8,20,128]{2,1,0:T(8,128)S(1)}, f32[8...) custom-call(f32[640,128]{1,0:T(8,128)} %bitcast.8, ...), custom_call_target="tpu_custom_call" | custom-call | flops 8192000 | bytes 3171328 | tf_op jit(solution)/shard_map/wrap_down/pallas_call | solution.py:612
  2.2 0.5 %collective-permute-start.1 = (f32[100,128]{1,0:T(8,128)S(1)}, f32[100,128]{1,0:T(8,128)S(1)}, u32[]{:S(2)}, u32[]{:S(2)}) collective-permute-start(f32[100,128]{1,0:T(8,128)S(1)} %get-tuple-element.53.own), channel_id=1, source_target_pairs={{0,4},{4,0},{8,12},{12,8},{16,20},{20,16},{24,28},{28,24},{1,5},{5... | collective-permute-start | bytes 153608 | tf_op jit(solution)/shard_map/ppermute | solution.py:637
  2.7 0.7 %wall_matrix.1 = (f32[160,128]{1,0:T(8,128)S(1)}, f32[6,16,128]{2,1,0:T(8,128)S(1)}, f32[24,80,128]{2,1,0:T(8,128)S(1)}, f32[27,80,128]{2,1,0:T(8,128)S(1)}, f32...) custom-call(f32[640,128]{1,0:T(8,128)S(1)} %get-tuple-element.47.ref, ...), custom_call_target="tpu_custom_call" | custom-call | flops 8192000 | bytes 3330048 | tf_op jit(solution)/shard_map/wall_matrix/pallas_call | solution.py:612
  3.5 2.7 %collective-permute-start = (f32[160,128]{1,0:T(8,128)S(1)}, f32[160,128]{1,0:T(8,128)S(1)}, u32[]{:S(2)}, u32[]{:S(2)}) collective-permute-start(f32[160,128]{1,0:T(8,128)S(1)} %get-tuple-element.49.own), channel_id=1, source_target_pairs={{0,1},{1,0},{2,3},{3,2},{4,5},{5,4},{6,7},{7,6},{8,9},{9,8},{10,11... | collective-permute-start | bytes 245768 | tf_op jit(solution)/shard_map/ppermute | solution.py:637
  6.1 0.0 collective-permute-done.1.other
  6.2 1.4 %collective-permute-start.3 = (f32[100,128]{1,0:T(8,128)S(1)}, f32[100,128]{1,0:T(8,128)S(1)}, u32[]{:S(2)}, u32[]{:S(2)}) collective-permute-start(f32[100,128]{1,0:T(8,128)S(1)} %get-tuple-element.55.own), channel_id=1, source_target_pairs={{0,12},{4,8},{8,20},{12,16},{16,28},{20,24},{24,4},{28,0},{1,13},{... | collective-permute-start | bytes 153608 | tf_op jit(solution)/shard_map/ppermute | solution.py:647
  7.5 1.3 %collective-permute-start.2 = (f32[100,128]{1,0:T(8,128)S(1)}, f32[100,128]{1,0:T(8,128)S(1)}, u32[]{:S(2)}, u32[]{:S(2)}) collective-permute-start(f32[100,128]{1,0:T(8,128)S(1)} %get-tuple-element.55.own), channel_id=1, source_target_pairs={{0,28},{4,24},{8,4},{12,0},{16,12},{20,8},{24,20},{28,16},{1,29},{... | collective-permute-start | bytes 153608 | tf_op jit(solution)/shard_map/ppermute | solution.py:647
  8.9 1.3 %collective-permute-start.4 = (f32[100,128]{1,0:T(8,128)S(1)}, f32[100,128]{1,0:T(8,128)S(1)}, u32[]{:S(2)}, u32[]{:S(2)}) collective-permute-start(f32[100,128]{1,0:T(8,128)S(1)} %get-tuple-element.55.own), channel_id=1, source_target_pairs={{0,20},{4,16},{8,28},{12,24},{16,4},{20,0},{24,12},{28,8},{1,21},{... | collective-permute-start | bytes 153608 | tf_op jit(solution)/shard_map/ppermute | solution.py:647
  10.2 0.0 collective-permute-done.other
  10.2 1.3 %wall_round_0.1 = (f32[40,128]{1,0:T(8,128)S(1)}, f32[8,10,128]{2,1,0:T(8,128)S(1)}, f32[12,10,128]{2,1,0:T(8,128)S(1)}, f32[12,10,128]{2,1,0:T(8,128)S(1)}, bf16[25,128,128]{2,1,0:T(8,128)(2,1)S(1)}) custom-call(f32[160,128]{1,0:T(8,128)S(1)} %get-tuple-element.49.own, f32[160,128]{1,0:T(8,128)S(1)} %collective-permute-done.other, bf16[25,128,128]{2,1,0:T(8,128)(2,1)} %bitcast.7), custom_call_target="tpu_custom_call" | custom-call | flops 256000 | bytes 2805760 | tf_op jit(solution)/shard_map/wall_round_0/pallas_call | solution.py:612
  11.5 0.0 collective-permute-done.3.before
  11.5 0.6 %collective-permute-done.2.following = f32[100,128]{1,0:T(8,128)S(1)} collective-permute-done((f32[100,128]{1,0:T(8,128)S(1)}, f32[100,128]{1,0:T(8,128)S(1)}, u32[]{:S(2)}, u32[]{:S(2)}) %collective-permute-start.2) | collective-permute-done | bytes 51232 | tf_op jit(solution)/shard_map/ppermute | solution.py:647
  12.2 0.5 %collective-permute-done.4.refs_1_ = f32[100,128]{1,0:T(8,128)S(1)} collective-permute-done((f32[100,128]{1,0:T(8,128)S(1)}, f32[100,128]{1,0:T(8,128)S(1)}, u32[]{:S(2)}, u32[]{:S(2)}) %collective-permute-start.4) | collective-permute-done | bytes 51232 | tf_op jit(solution)/shard_map/ppermute | solution.py:647
  12.7 0.6 %middle.1 = (f32[40,128]{1,0:T(8,128)S(1)}, f32[6,80,128]{2,1,0:T(8,128)S(1)}, f32[2,40,128]{2,1,0:T(8,128)S(1)}, f32[2,20,128]{2,1,0:T(8,128)S(1)}, f32[2,10,128]{2,1,0:T(8,128)S(1)}) custom-call(f32[100,128]{1,0:T(8,128)S(1)} %get-tuple-element.56.refs_0_, f32[100,128]{1,0:T(8,128)S(1)} %collective-permute-done.4.refs_1_, ...), custom_call_target="tpu_custom_call" | custom-call | flops 8192000 | bytes 4534272 | tf_op jit(solution)/shard_map/middle/pallas_call | solution.py:612
  13.4 2.6 %collective-permute-start.5 = (f32[60,128]{1,0:T(8,128)S(1)}, f32[60,128]{1,0:T(8,128)S(1)}, u32[]{:S(2)}, u32[]{:S(2)}) collective-permute-start(f32[60,128]{1,0:T(8,128)S(1)} %get-tuple-element.78), channel_id=1, source_target_pairs={{0,2},{1,3},{2,1},{3,0},{4,6},{5,7},{6,5},{7,4},{8,10},{9,11},{10,... | collective-permute-start | bytes 92168 | tf_op jit(solution)/shard_map/ppermute | solution.py:647
  16.0 1.2 %collective-permute-start.7 = (f32[40,128]{1,0:T(8,128)S(1)}, f32[40,128]{1,0:T(8,128)S(1)}, u32[]{:S(2)}, u32[]{:S(2)}) collective-permute-start(f32[40,128]{1,0:T(8,128)S(1)} %get-tuple-element.79), channel_id=1, source_target_pairs={{0,3},{1,2},{2,0},{3,1},{4,7},{5,6},{6,4},{7,5},{8,11},{9,10},{10,... | collective-permute-start | bytes 61448 | tf_op jit(solution)/shard_map/ppermute | solution.py:647
  17.2 0.0 collective-permute-start.6
  17.2 3.5 %collective-permute-done.7.refs_6_ = f32[40,128]{1,0:T(8,128)S(1)} collective-permute-done((f32[40,128]{1,0:T(8,128)S(1)}, f32[40,128]{1,0:T(8,128)S(1)}, u32[]{:S(2)}, u32[]{:S(2)}) %collective-permute-start.7) | collective-permute-done | bytes 20512 | tf_op jit(solution)/shard_map/ppermute | solution.py:647
  20.8 0.2 %collective-permute-done.6.refs_5_ = f32[40,128]{1,0:T(8,128)S(1)} collective-permute-done((f32[40,128]{1,0:T(8,128)S(1)}, f32[40,128]{1,0:T(8,128)S(1)}, u32[]{:S(2)}, u32[]{:S(2)}) %collective-permute-start.6) | collective-permute-done | bytes 20512 | tf_op jit(solution)/shard_map/ppermute | solution.py:637
  21.0 0.0 collective-permute-done.5.refs_4_
  21.0 0.9 %wall_up.1 = f32[640,128]{1,0:T(8,128)} custom-call(f32[40,128]{1,0:T(8,128)S(1)} %get-tuple-element.50.matrix.refs_0_, f32[12,10,128]{2,1,0:T(8,128)S(1)} %get-tuple-element.51.down_in.refs_1_, f32[12,10,128]{2,1,0:T(8,128)S(1)} %get-tuple-element.52.outer_in.refs_2_, f32[40,128]{1,0:T(8,128)S(1)} %get-tuple-element.77.refs_3_, ...), custom_call_target="tpu_custom_call" | custom-call | flops 2457600 | bytes 2191360 | tf_op jit(solution)/shard_map/wall_up/pallas_call | solution.py:612
  (3 shorter events, 0.1 us)
Async XLA Ops:
  2.2 3.9 %collective-permute-start.1 = (f32[100,128]{1,0:T(8,128)S(1)}, f32[100,128]{1,0:T(8,128)S(1)}, u32[]{:S(2)}, u32[]{:S(2)}) collective-permute-start(f32[100,128]{1,0:T(8,128)S(1)} %get-tuple-element.53.own), channel_id=1, source_target_pairs={{0,4},{4,0},{8,12},{12,8},{16,20},{20,16},{24,28},{28,24},{1,5},{5... | collective-permute-start | bytes 153608 | tf_op jit(solution)/shard_map/ppermute | solution.py:637
  3.5 6.7 %collective-permute-start = (f32[160,128]{1,0:T(8,128)S(1)}, f32[160,128]{1,0:T(8,128)S(1)}, u32[]{:S(2)}, u32[]{:S(2)}) collective-permute-start(f32[160,128]{1,0:T(8,128)S(1)} %get-tuple-element.49.own), channel_id=1, source_target_pairs={{0,1},{1,0},{2,3},{3,2},{4,5},{5,4},{6,7},{7,6},{8,9},{9,8},{10,11... | collective-permute-start | bytes 245768 | tf_op jit(solution)/shard_map/ppermute | solution.py:637
  6.2 5.3 %collective-permute-start.3 = (f32[100,128]{1,0:T(8,128)S(1)}, f32[100,128]{1,0:T(8,128)S(1)}, u32[]{:S(2)}, u32[]{:S(2)}) collective-permute-start(f32[100,128]{1,0:T(8,128)S(1)} %get-tuple-element.55.own), channel_id=1, source_target_pairs={{0,12},{4,8},{8,20},{12,16},{16,28},{20,24},{24,4},{28,0},{1,13},{... | collective-permute-start | bytes 153608 | tf_op jit(solution)/shard_map/ppermute | solution.py:647
  7.5 4.6 %collective-permute-start.2 = (f32[100,128]{1,0:T(8,128)S(1)}, f32[100,128]{1,0:T(8,128)S(1)}, u32[]{:S(2)}, u32[]{:S(2)}) collective-permute-start(f32[100,128]{1,0:T(8,128)S(1)} %get-tuple-element.55.own), channel_id=1, source_target_pairs={{0,28},{4,24},{8,4},{12,0},{16,12},{20,8},{24,20},{28,16},{1,29},{... | collective-permute-start | bytes 153608 | tf_op jit(solution)/shard_map/ppermute | solution.py:647
  8.9 3.8 %collective-permute-start.4 = (f32[100,128]{1,0:T(8,128)S(1)}, f32[100,128]{1,0:T(8,128)S(1)}, u32[]{:S(2)}, u32[]{:S(2)}) collective-permute-start(f32[100,128]{1,0:T(8,128)S(1)} %get-tuple-element.55.own), channel_id=1, source_target_pairs={{0,20},{4,16},{8,28},{12,24},{16,4},{20,0},{24,12},{28,8},{1,21},{... | collective-permute-start | bytes 153608 | tf_op jit(solution)/shard_map/ppermute | solution.py:647
  13.4 7.7 %collective-permute-start.5 = (f32[60,128]{1,0:T(8,128)S(1)}, f32[60,128]{1,0:T(8,128)S(1)}, u32[]{:S(2)}, u32[]{:S(2)}) collective-permute-start(f32[60,128]{1,0:T(8,128)S(1)} %get-tuple-element.78), channel_id=1, source_target_pairs={{0,2},{1,3},{2,1},{3,0},{4,6},{5,7},{6,5},{7,4},{8,10},{9,11},{10,... | collective-permute-start | bytes 92168 | tf_op jit(solution)/shard_map/ppermute | solution.py:647
  16.0 4.8 %collective-permute-start.7 = (f32[40,128]{1,0:T(8,128)S(1)}, f32[40,128]{1,0:T(8,128)S(1)}, u32[]{:S(2)}, u32[]{:S(2)}) collective-permute-start(f32[40,128]{1,0:T(8,128)S(1)} %get-tuple-element.79), channel_id=1, source_target_pairs={{0,3},{1,2},{2,0},{3,1},{4,7},{5,6},{6,4},{7,5},{8,11},{9,10},{10,... | collective-permute-start | bytes 61448 | tf_op jit(solution)/shard_map/ppermute | solution.py:647
  17.2 3.8 %collective-permute-start.6 = (f32[40,128]{1,0:T(8,128)S(1)}, f32[40,128]{1,0:T(8,128)S(1)}, u32[]{:S(2)}, u32[]{:S(2)}) collective-permute-start(f32[40,128]{1,0:T(8,128)S(1)} %get-tuple-element.77.refs_3_), channel_id=1, source_target_pairs={{0,1},{1,0},{2,3},{3,2},{4,5},{5,4},{6,7},{7,6},{8,9},{9,8},{10,11... | collective-permute-start | bytes 61448 | tf_op jit(solution)/shard_map/ppermute | solution.py:637
where the time goes:
time: 22.1 us; the launch traced here: 21.9 us
  starting transfers between devices  11.1 us (50%)
  Pallas kernels  5.83 us (26%)
  waiting for transfers between devices  4.92 us (22%)
    ppermute x5, starting transfers between devices, pass_on(): return lax.ppermute(array, axis, [(i, target(i)) for i in range(count)])  7.91 us
    pallas_call x8, Pallas kernels, kernel(): pl.pallas_call(body, out_shape=[a for a, _ in outs], in_specs=[spec for _...  5.83 us
    ppermute x5, waiting for transfers between devices, pass_on(): return lax.ppermute(array, axis, [(i, target(i)) for i in range(count)])  4.68 us
    ppermute x3, starting transfers between devices, exchange(): return lax.ppermute(array, axis, [(i, i ^ mask) for i in range(count)])  3.17 us
  transfers between devices with their start and end apart: 8, of which 4 were waited for; matrix products, arithmetic and copies ran while one was open for 0% of the time, Pallas kernels for 10%

commit v1 on v0

--- a/solution.py
+++ b/solution.py
@@ -447,18 +447,19 @@
     return minus(centre, apply(factors[8:12], outer)), outer, w
 
 
-def wall_share(lines, bit, own, down_in, outer_in, matrix, share, bundle, copy):
-    share[pl.ds(2 * lines, 2 * lines), :] = jnp.zeros((2 * lines, share.shape[1]), jnp.float32)
+def wall_share(lines, bit, own, down_in, outer_in, matrix, share_one, share_two, copy):
     copy[...] = own[...]
-    bundle[pl.ds(2 * lines, 4 * lines), :] = matrix[...]
+    half = pl.ds(2 * lines, 2 * lines)
+    share_one[half, :] = matrix[pl.ds(0, 2 * lines), :]
+    share_two[half, :] = matrix[half, :]
     second, upper = is_second("normal", bit), is_second("normal", bit + 1)
     for at, size in blocks(lines, 8):
         mine = flat(own, SOURCE, lines, at, size)
         none = tuple(jnp.zeros_like(value) for value in mine)
         down, factors = get(down_in, MERGE_DOWN, at, size), get(outer_in, 12, at, size)
         part, _, _ = reduce_source(down, factors, second, upper, mine, none)
-        put_flat(share, part, lines, at, size)
-        put_flat(bundle, part, lines, at, size)
+        put_flat(share_one, part, lines, at, size)
+        put_flat(share_two, part, lines, at, size)
 
 
 def wrap_three(fields, own, following, before, packed, back_up, back_w, next_up, next_w):
@@ -546,7 +547,7 @@
 
 
 def wall_up(fields, span, cells, bits, *refs):
-    own_matrix, down_in, outer_in, own, bundle, other, share = refs[0:7]
+    own_matrix, down_in, outer_in, own, other, share_two, share_one = refs[0:7]
     refs = refs[7:]
     round_ups, round_ws, refs = refs[: bits + 1], refs[bits + 1 : 2 * bits + 1], refs[2 * bits + 1 :]
     chunk_up, chunk_w, ups, ws = refs[0], refs[1], refs[2:5], refs[5:8]
@@ -564,9 +565,9 @@
             flat(own, SOURCE, lines, at, size),
             flat(other, SOURCE, lines, at, size),
         )
-        opposite = flat(bundle, 6, lines, at, size)
-        shares = plus(opposite[0:2], flat(share, 2, lines, at, size))
-        matrix = plus(flat(own_matrix, 4, lines, at, size), opposite[2:6])
+        one, two = (flat(share, 4, lines, at, size) for share in (share_one, share_two))
+        shares = plus(one[0:2], two[0:2])
+        matrix = plus(flat(own_matrix, 4, lines, at, size), one[2:4] + two[2:4])
         centre = apply(inverse(*matrix), plus(part, shares))
         outer = minus(outer, apply(factors[0:4], apply(factors[4:8], centre)))
         left, right = choose(upper, centre, outer), choose(upper, outer, centre)
@@ -795,11 +796,11 @@
             50 * lines * wide,
         )
         round_ws.append(w)
-    share, bundle, source = kernel(
+    share_one, share_two, source = kernel(
         "wall_share",
         functools.partial(wall_share, lines, wall_bits),
         inside([source, round_downs[wall_bits]] + outer + [matrix]),
-        inside([f32(SOURCE * lines, wide), f32(6 * lines, wide), f32(SOURCE * lines, wide)]),
+        inside([f32(SOURCE * lines, wide)] * 3),
         [],
         50 * lines * wide,
     )
@@ -811,9 +812,9 @@
             + outer
             + [
                 source,
-                pass_on(bundle, "normal", wall_bits, (2, 3, 1, 0)),
                 exchange(source, "normal", 1 << wall_bits),
-                pass_on(share, "normal", wall_bits, (3, 2, 0, 1)),
+                pass_on(share_two, "normal", wall_bits, (3, 2, 0, 1)),
+                pass_on(share_one, "normal", wall_bits, (2, 3, 1, 0)),
             ]
             + round_ups
             + round_ws

time: 22.1 us -> 22.5 us (1.018)
  waiting for transfers between devices: 4.92 us -> 5.88 us
  starting transfers between devices: 11.1 us -> 10.6 us
    ppermute x5, waiting for transfers between devices: 4.68 us -> 5.87 us  [pass_on(): return lax.ppermute(array, axis, [(i, target(i)) for i in range(count)])]
    ppermute x5, starting transfers between devices: 7.91 us -> 7.01 us  [pass_on(): return lax.ppermute(array, axis, [(i, target(i)) for i in range(count)])]
    ppermute x3, starting transfers between devices: 3.17 us -> 3.56 us  [exchange(): return lax.ppermute(array, axis, [(i, i ^ mask) for i in range(count)])]
    ppermute x3, waiting for transfers between devices: 0.24 us -> 0.01 us  [exchange(): return lax.ppermute(array, axis, [(i, i ^ mask) for i in range(count)])]
  transfers between devices with their start and end apart: 8 -> 8, of which waited for: 4 -> 4; matrix products, arithmetic and copies ran while one was open for 0% -> 0% of each run, Pallas kernels for 10% -> 9%
where the time goes in v1:
time: 22.5 us; the launch traced here: 22.3 us
  starting transfers between devices  10.6 us (47%)
  waiting for transfers between devices  5.88 us (26%)
  Pallas kernels  5.83 us (26%)
    ppermute x5, starting transfers between devices, pass_on(): return lax.ppermute(array, axis, [(i, target(i)) for i in range(count)])  7.01 us
    ppermute x5, waiting for transfers between devices, pass_on(): return lax.ppermute(array, axis, [(i, target(i)) for i in range(count)])  5.87 us
    pallas_call x8, Pallas kernels, kernel(): pl.pallas_call(body, out_shape=[a for a, _ in outs], in_specs=[spec for _...  5.83 us
    ppermute x3, starting transfers between devices, exchange(): return lax.ppermute(array, axis, [(i, i ^ mask) for i in range(count)])  3.56 us
  transfers between devices with their start and end apart: 8, of which 4 were waited for; matrix products, arithmetic and copies ran while one was open for 0% of the time, Pallas kernels for 9%

profile of v1, /device:TPU:0, one launch (start us, length us, event | category | flops | bytes accessed | tf_op | source)
XLA Modules:
  0.0 22.3 jit_solution(2993045773256090013)
XLA Ops:
  0.0 2.2 %wrap_down.1 = (f32[100,128]{1,0:T(8,128)S(1)}, f32[56,40,128]{2,1,0:T(8,128)S(1)}, f32[14,40,128]{2,1,0:T(8,128)S(1)}, f32[8,20,128]{2,1,0:T(8,128)S(1)}, f32[8...) custom-call(f32[640,128]{1,0:T(8,128)} %bitcast.8, ...), custom_call_target="tpu_custom_call" | custom-call | flops 8192000 | bytes 3171328 | tf_op jit(solution)/shard_map/wrap_down/pallas_call | solution.py:613
  2.2 0.5 %collective-permute-start.1 = (f32[100,128]{1,0:T(8,128)S(1)}, f32[100,128]{1,0:T(8,128)S(1)}, u32[]{:S(2)}, u32[]{:S(2)}) collective-permute-start(f32[100,128]{1,0:T(8,128)S(1)} %get-tuple-element.53.own), channel_id=1, source_target_pairs={{0,4},{4,0},{8,12},{12,8},{16,20},{20,16},{24,28},{28,24},{1,5},{5... | collective-permute-start | bytes 153608 | tf_op jit(solution)/shard_map/ppermute | solution.py:638
  2.7 0.7 %wall_matrix.1 = (f32[160,128]{1,0:T(8,128)S(1)}, f32[6,16,128]{2,1,0:T(8,128)S(1)}, f32[24,80,128]{2,1,0:T(8,128)S(1)}, f32[27,80,128]{2,1,0:T(8,128)S(1)}, f32...) custom-call(f32[640,128]{1,0:T(8,128)S(1)} %get-tuple-element.47.ref, ...), custom_call_target="tpu_custom_call" | custom-call | flops 8192000 | bytes 3330048 | tf_op jit(solution)/shard_map/wall_matrix/pallas_call | solution.py:613
  3.5 2.7 %collective-permute-start = (f32[160,128]{1,0:T(8,128)S(1)}, f32[160,128]{1,0:T(8,128)S(1)}, u32[]{:S(2)}, u32[]{:S(2)}) collective-permute-start(f32[160,128]{1,0:T(8,128)S(1)} %get-tuple-element.49.own), channel_id=1, source_target_pairs={{0,1},{1,0},{2,3},{3,2},{4,5},{5,4},{6,7},{7,6},{8,9},{9,8},{10,11... | collective-permute-start | bytes 245768 | tf_op jit(solution)/shard_map/ppermute | solution.py:638
  6.1 0.0 collective-permute-done.1.other
  6.2 1.4 %collective-permute-start.3 = (f32[100,128]{1,0:T(8,128)S(1)}, f32[100,128]{1,0:T(8,128)S(1)}, u32[]{:S(2)}, u32[]{:S(2)}) collective-permute-start(f32[100,128]{1,0:T(8,128)S(1)} %get-tuple-element.55.own), channel_id=1, source_target_pairs={{0,12},{4,8},{8,20},{12,16},{16,28},{20,24},{24,4},{28,0},{1,13},{... | collective-permute-start | bytes 153608 | tf_op jit(solution)/shard_map/ppermute | solution.py:648
  7.5 1.3 %collective-permute-start.2 = (f32[100,128]{1,0:T(8,128)S(1)}, f32[100,128]{1,0:T(8,128)S(1)}, u32[]{:S(2)}, u32[]{:S(2)}) collective-permute-start(f32[100,128]{1,0:T(8,128)S(1)} %get-tuple-element.55.own), channel_id=1, source_target_pairs={{0,28},{4,24},{8,4},{12,0},{16,12},{20,8},{24,20},{28,16},{1,29},{... | collective-permute-start | bytes 153608 | tf_op jit(solution)/shard_map/ppermute | solution.py:648
  8.9 1.3 %collective-permute-start.4 = (f32[100,128]{1,0:T(8,128)S(1)}, f32[100,128]{1,0:T(8,128)S(1)}, u32[]{:S(2)}, u32[]{:S(2)}) collective-permute-start(f32[100,128]{1,0:T(8,128)S(1)} %get-tuple-element.55.own), channel_id=1, source_target_pairs={{0,20},{4,16},{8,28},{12,24},{16,4},{20,0},{24,12},{28,8},{1,21},{... | collective-permute-start | bytes 153608 | tf_op jit(solution)/shard_map/ppermute | solution.py:648
  10.2 0.0 collective-permute-done.other
  10.2 1.3 %wall_round_0.1 = (f32[40,128]{1,0:T(8,128)S(1)}, f32[8,10,128]{2,1,0:T(8,128)S(1)}, f32[12,10,128]{2,1,0:T(8,128)S(1)}, f32[12,10,128]{2,1,0:T(8,128)S(1)}, bf16[25,128,128]{2,1,0:T(8,128)(2,1)S(1)}) custom-call(f32[160,128]{1,0:T(8,128)S(1)} %get-tuple-element.49.own, f32[160,128]{1,0:T(8,128)S(1)} %collective-permute-done.other, bf16[25,128,128]{2,1,0:T(8,128)(2,1)} %bitcast.7), custom_call_target="tpu_custom_call" | custom-call | flops 256000 | bytes 2805760 | tf_op jit(solution)/shard_map/wall_round_0/pallas_call | solution.py:613
  11.5 0.0 collective-permute-done.3.before
  11.5 0.6 %collective-permute-done.2.following = f32[100,128]{1,0:T(8,128)S(1)} collective-permute-done((f32[100,128]{1,0:T(8,128)S(1)}, f32[100,128]{1,0:T(8,128)S(1)}, u32[]{:S(2)}, u32[]{:S(2)}) %collective-permute-start.2) | collective-permute-done | bytes 51232 | tf_op jit(solution)/shard_map/ppermute | solution.py:648
  12.2 0.5 %collective-permute-done.4.refs_1_ = f32[100,128]{1,0:T(8,128)S(1)} collective-permute-done((f32[100,128]{1,0:T(8,128)S(1)}, f32[100,128]{1,0:T(8,128)S(1)}, u32[]{:S(2)}, u32[]{:S(2)}) %collective-permute-start.4) | collective-permute-done | bytes 51232 | tf_op jit(solution)/shard_map/ppermute | solution.py:648
  12.7 0.6 %middle.1 = (f32[40,128]{1,0:T(8,128)S(1)}, f32[6,80,128]{2,1,0:T(8,128)S(1)}, f32[2,40,128]{2,1,0:T(8,128)S(1)}, f32[2,20,128]{2,1,0:T(8,128)S(1)}, f32[2,10,128]{2,1,0:T(8,128)S(1)}) custom-call(f32[100,128]{1,0:T(8,128)S(1)} %get-tuple-element.56.refs_0_, f32[100,128]{1,0:T(8,128)S(1)} %collective-permute-done.4.refs_1_, ...), custom_call_target="tpu_custom_call" | custom-call | flops 8192000 | bytes 4534272 | tf_op jit(solution)/shard_map/middle/pallas_call | solution.py:613
  13.4 2.5 %collective-permute-start.6 = (f32[40,128]{1,0:T(8,128)S(1)}, f32[40,128]{1,0:T(8,128)S(1)}, u32[]{:S(2)}, u32[]{:S(2)}) collective-permute-start(f32[40,128]{1,0:T(8,128)S(1)} %get-tuple-element.78), channel_id=1, source_target_pairs={{0,3},{1,2},{2,0},{3,1},{4,7},{5,6},{6,4},{7,5},{8,11},{9,10},{10,... | collective-permute-start | bytes 61448 | tf_op jit(solution)/shard_map/ppermute | solution.py:648
  15.9 0.5 %collective-permute-start.7 = (f32[40,128]{1,0:T(8,128)S(1)}, f32[40,128]{1,0:T(8,128)S(1)}, u32[]{:S(2)}, u32[]{:S(2)}) collective-permute-start(f32[40,128]{1,0:T(8,128)S(1)} %get-tuple-element.79), channel_id=1, source_target_pairs={{0,2},{1,3},{2,1},{3,0},{4,6},{5,7},{6,5},{7,4},{8,10},{9,11},{10,... | collective-permute-start | bytes 61448 | tf_op jit(solution)/shard_map/ppermute | solution.py:648
  16.3 0.4 %collective-permute-start.5 = (f32[40,128]{1,0:T(8,128)S(1)}, f32[40,128]{1,0:T(8,128)S(1)}, u32[]{:S(2)}, u32[]{:S(2)}) collective-permute-start(f32[40,128]{1,0:T(8,128)S(1)} %get-tuple-element.77.refs_3_), channel_id=1, source_target_pairs={{0,1},{1,0},{2,3},{3,2},{4,5},{5,4},{6,7},{7,6},{8,9},{9,8},{10,11... | collective-permute-start | bytes 61448 | tf_op jit(solution)/shard_map/ppermute | solution.py:638
  16.7 1.4 %collective-permute-done.6.refs_5_ = f32[40,128]{1,0:T(8,128)S(1)} collective-permute-done((f32[40,128]{1,0:T(8,128)S(1)}, f32[40,128]{1,0:T(8,128)S(1)}, u32[]{:S(2)}, u32[]{:S(2)}) %collective-permute-start.6) | collective-permute-done | bytes 20512 | tf_op jit(solution)/shard_map/ppermute | solution.py:648
  18.1 3.3 %collective-permute-done.7.refs_6_ = f32[40,128]{1,0:T(8,128)S(1)} collective-permute-done((f32[40,128]{1,0:T(8,128)S(1)}, f32[40,128]{1,0:T(8,128)S(1)}, u32[]{:S(2)}, u32[]{:S(2)}) %collective-permute-start.7) | collective-permute-done | bytes 20512 | tf_op jit(solution)/shard_map/ppermute | solution.py:648
  21.5 0.0 collective-permute-done.5.refs_4_
  21.5 0.9 %wall_up.1 = f32[640,128]{1,0:T(8,128)} custom-call(f32[40,128]{1,0:T(8,128)S(1)} %get-tuple-element.50.matrix.refs_0_, f32[12,10,128]{2,1,0:T(8,128)S(1)} %get-tuple-element.51.down_in.refs_1_, f32[12,10,128]{2,1,0:T(8,128)S(1)} %get-tuple-element.52.outer_in.refs_2_, f32[40,128]{1,0:T(8,128)S(1)} %get-tuple-element.77.refs_3_, ...), custom_call_target="tpu_custom_call" | custom-call | flops 2457600 | bytes 2181120 | tf_op jit(solution)/shard_map/wall_up/pallas_call | solution.py:613
  (3 shorter events, 0.1 us)
Async XLA Ops:
  2.2 3.9 %collective-permute-start.1 = (f32[100,128]{1,0:T(8,128)S(1)}, f32[100,128]{1,0:T(8,128)S(1)}, u32[]{:S(2)}, u32[]{:S(2)}) collective-permute-start(f32[100,128]{1,0:T(8,128)S(1)} %get-tuple-element.53.own), channel_id=1, source_target_pairs={{0,4},{4,0},{8,12},{12,8},{16,20},{20,16},{24,28},{28,24},{1,5},{5... | collective-permute-start | bytes 153608 | tf_op jit(solution)/shard_map/ppermute | solution.py:638
  3.5 6.7 %collective-permute-start = (f32[160,128]{1,0:T(8,128)S(1)}, f32[160,128]{1,0:T(8,128)S(1)}, u32[]{:S(2)}, u32[]{:S(2)}) collective-permute-start(f32[160,128]{1,0:T(8,128)S(1)} %get-tuple-element.49.own), channel_id=1, source_target_pairs={{0,1},{1,0},{2,3},{3,2},{4,5},{5,4},{6,7},{7,6},{8,9},{9,8},{10,11... | collective-permute-start | bytes 245768 | tf_op jit(solution)/shard_map/ppermute | solution.py:638
  6.2 5.3 %collective-permute-start.3 = (f32[100,128]{1,0:T(8,128)S(1)}, f32[100,128]{1,0:T(8,128)S(1)}, u32[]{:S(2)}, u32[]{:S(2)}) collective-permute-start(f32[100,128]{1,0:T(8,128)S(1)} %get-tuple-element.55.own), channel_id=1, source_target_pairs={{0,12},{4,8},{8,20},{12,16},{16,28},{20,24},{24,4},{28,0},{1,13},{... | collective-permute-start | bytes 153608 | tf_op jit(solution)/shard_map/ppermute | solution.py:648
  7.5 4.6 %collective-permute-start.2 = (f32[100,128]{1,0:T(8,128)S(1)}, f32[100,128]{1,0:T(8,128)S(1)}, u32[]{:S(2)}, u32[]{:S(2)}) collective-permute-start(f32[100,128]{1,0:T(8,128)S(1)} %get-tuple-element.55.own), channel_id=1, source_target_pairs={{0,28},{4,24},{8,4},{12,0},{16,12},{20,8},{24,20},{28,16},{1,29},{... | collective-permute-start | bytes 153608 | tf_op jit(solution)/shard_map/ppermute | solution.py:648
  8.9 3.8 %collective-permute-start.4 = (f32[100,128]{1,0:T(8,128)S(1)}, f32[100,128]{1,0:T(8,128)S(1)}, u32[]{:S(2)}, u32[]{:S(2)}) collective-permute-start(f32[100,128]{1,0:T(8,128)S(1)} %get-tuple-element.55.own), channel_id=1, source_target_pairs={{0,20},{4,16},{8,28},{12,24},{16,4},{20,0},{24,12},{28,8},{1,21},{... | collective-permute-start | bytes 153608 | tf_op jit(solution)/shard_map/ppermute | solution.py:648
  13.4 4.8 %collective-permute-start.6 = (f32[40,128]{1,0:T(8,128)S(1)}, f32[40,128]{1,0:T(8,128)S(1)}, u32[]{:S(2)}, u32[]{:S(2)}) collective-permute-start(f32[40,128]{1,0:T(8,128)S(1)} %get-tuple-element.78), channel_id=1, source_target_pairs={{0,3},{1,2},{2,0},{3,1},{4,7},{5,6},{6,4},{7,5},{8,11},{9,10},{10,... | collective-permute-start | bytes 61448 | tf_op jit(solution)/shard_map/ppermute | solution.py:648
  15.9 5.6 %collective-permute-start.7 = (f32[40,128]{1,0:T(8,128)S(1)}, f32[40,128]{1,0:T(8,128)S(1)}, u32[]{:S(2)}, u32[]{:S(2)}) collective-permute-start(f32[40,128]{1,0:T(8,128)S(1)} %get-tuple-element.79), channel_id=1, source_target_pairs={{0,2},{1,3},{2,1},{3,0},{4,6},{5,7},{6,5},{7,4},{8,10},{9,11},{10,... | collective-permute-start | bytes 61448 | tf_op jit(solution)/shard_map/ppermute | solution.py:648
  16.3 5.1 %collective-permute-start.5 = (f32[40,128]{1,0:T(8,128)S(1)}, f32[40,128]{1,0:T(8,128)S(1)}, u32[]{:S(2)}, u32[]{:S(2)}) collective-permute-start(f32[40,128]{1,0:T(8,128)S(1)} %get-tuple-element.77.refs_3_), channel_id=1, source_target_pairs={{0,1},{1,0},{2,3},{3,2},{4,5},{5,4},{6,7},{7,6},{8,9},{9,8},{10,11... | collective-permute-start | bytes 61448 | tf_op jit(solution)/shard_map/ppermute | solution.py:638

commit v2 on v1

--- a/solution.py
+++ b/solution.py
@@ -813,8 +813,8 @@
             + [
                 source,
                 exchange(source, "normal", 1 << wall_bits),
-                pass_on(share_two, "normal", wall_bits, (3, 2, 0, 1)),
-                pass_on(share_one, "normal", wall_bits, (2, 3, 1, 0)),
+                pass_on(share_two, "normal", wall_bits, (2, 3, 1, 0)),
+                pass_on(share_one, "normal", wall_bits, (3, 2, 0, 1)),
             ]
             + round_ups
             + round_ws

time: 22.5 us -> 22 us (0.978)
  waiting for transfers between devices: 5.88 us -> 4.91 us
  starting transfers between devices: 10.6 us -> 11.1 us
    ppermute x5, waiting for transfers between devices: 5.87 us -> 4.68 us  [pass_on(): return lax.ppermute(array, axis, [(i, target(i)) for i in range(count)])]
    ppermute x5, starting transfers between devices: 7.01 us -> 7.91 us  [pass_on(): return lax.ppermute(array, axis, [(i, target(i)) for i in range(count)])]
    ppermute x3, starting transfers between devices: 3.56 us -> 3.17 us  [exchange(): return lax.ppermute(array, axis, [(i, i ^ mask) for i in range(count)])]
    ppermute x3, waiting for transfers between devices: 0.01 us -> 0.24 us  [exchange(): return lax.ppermute(array, axis, [(i, i ^ mask) for i in range(count)])]
  transfers between devices with their start and end apart: 8 -> 8, of which waited for: 4 -> 5; matrix products, arithmetic and copies ran while one was open for 0% -> 0% of each run, Pallas kernels for 9% -> 10%
where the time goes in v2:
time: 22 us; the launch traced here: 21.9 us
  starting transfers between devices  11.1 us (50%)
  Pallas kernels  5.83 us (26%)
  waiting for transfers between devices  4.91 us (22%)
    ppermute x5, starting transfers between devices, pass_on(): return lax.ppermute(array, axis, [(i, target(i)) for i in range(count)])  7.91 us
    pallas_call x8, Pallas kernels, kernel(): pl.pallas_call(body, out_shape=[a for a, _ in outs], in_specs=[spec for _...  5.83 us
    ppermute x5, waiting for transfers between devices, pass_on(): return lax.ppermute(array, axis, [(i, target(i)) for i in range(count)])  4.68 us
    ppermute x3, starting transfers between devices, exchange(): return lax.ppermute(array, axis, [(i, i ^ mask) for i in range(count)])  3.17 us
  transfers between devices with their start and end apart: 8, of which 5 were waited for; matrix products, arithmetic and copies ran while one was open for 0% of the time, Pallas kernels for 10%

profile of v2, /device:TPU:0, one launch (start us, length us, event | category | flops | bytes accessed | tf_op | source)
XLA Modules:
  0.0 21.9 jit_solution(9632439392830286671)
XLA Ops:
  0.0 2.2 %wrap_down.1 = (f32[100,128]{1,0:T(8,128)S(1)}, f32[56,40,128]{2,1,0:T(8,128)S(1)}, f32[14,40,128]{2,1,0:T(8,128)S(1)}, f32[8,20,128]{2,1,0:T(8,128)S(1)}, f32[8...) custom-call(f32[640,128]{1,0:T(8,128)} %bitcast.8, ...), custom_call_target="tpu_custom_call" | custom-call | flops 8192000 | bytes 3171328 | tf_op jit(solution)/shard_map/wrap_down/pallas_call | solution.py:613
  2.2 0.5 %collective-permute-start.1 = (f32[100,128]{1,0:T(8,128)S(1)}, f32[100,128]{1,0:T(8,128)S(1)}, u32[]{:S(2)}, u32[]{:S(2)}) collective-permute-start(f32[100,128]{1,0:T(8,128)S(1)} %get-tuple-element.53.own), channel_id=1, source_target_pairs={{0,4},{4,0},{8,12},{12,8},{16,20},{20,16},{24,28},{28,24},{1,5},{5... | collective-permute-start | bytes 153608 | tf_op jit(solution)/shard_map/ppermute | solution.py:638
  2.7 0.7 %wall_matrix.1 = (f32[160,128]{1,0:T(8,128)S(1)}, f32[6,16,128]{2,1,0:T(8,128)S(1)}, f32[24,80,128]{2,1,0:T(8,128)S(1)}, f32[27,80,128]{2,1,0:T(8,128)S(1)}, f32...) custom-call(f32[640,128]{1,0:T(8,128)S(1)} %get-tuple-element.47.ref, ...), custom_call_target="tpu_custom_call" | custom-call | flops 8192000 | bytes 3330048 | tf_op jit(solution)/shard_map/wall_matrix/pallas_call | solution.py:613
  3.5 2.7 %collective-permute-start = (f32[160,128]{1,0:T(8,128)S(1)}, f32[160,128]{1,0:T(8,128)S(1)}, u32[]{:S(2)}, u32[]{:S(2)}) collective-permute-start(f32[160,128]{1,0:T(8,128)S(1)} %get-tuple-element.49.own), channel_id=1, source_target_pairs={{0,1},{1,0},{2,3},{3,2},{4,5},{5,4},{6,7},{7,6},{8,9},{9,8},{10,11... | collective-permute-start | bytes 245768 | tf_op jit(solution)/shard_map/ppermute | solution.py:638
  6.1 0.0 collective-permute-done.1.other
  6.2 1.4 %collective-permute-start.3 = (f32[100,128]{1,0:T(8,128)S(1)}, f32[100,128]{1,0:T(8,128)S(1)}, u32[]{:S(2)}, u32[]{:S(2)}) collective-permute-start(f32[100,128]{1,0:T(8,128)S(1)} %get-tuple-element.55.own), channel_id=1, source_target_pairs={{0,12},{4,8},{8,20},{12,16},{16,28},{20,24},{24,4},{28,0},{1,13},{... | collective-permute-start | bytes 153608 | tf_op jit(solution)/shard_map/ppermute | solution.py:648
  7.5 1.3 %collective-permute-start.2 = (f32[100,128]{1,0:T(8,128)S(1)}, f32[100,128]{1,0:T(8,128)S(1)}, u32[]{:S(2)}, u32[]{:S(2)}) collective-permute-start(f32[100,128]{1,0:T(8,128)S(1)} %get-tuple-element.55.own), channel_id=1, source_target_pairs={{0,28},{4,24},{8,4},{12,0},{16,12},{20,8},{24,20},{28,16},{1,29},{... | collective-permute-start | bytes 153608 | tf_op jit(solution)/shard_map/ppermute | solution.py:648
  8.9 1.3 %collective-permute-start.4 = (f32[100,128]{1,0:T(8,128)S(1)}, f32[100,128]{1,0:T(8,128)S(1)}, u32[]{:S(2)}, u32[]{:S(2)}) collective-permute-start(f32[100,128]{1,0:T(8,128)S(1)} %get-tuple-element.55.own), channel_id=1, source_target_pairs={{0,20},{4,16},{8,28},{12,24},{16,4},{20,0},{24,12},{28,8},{1,21},{... | collective-permute-start | bytes 153608 | tf_op jit(solution)/shard_map/ppermute | solution.py:648
  10.2 0.0 collective-permute-done.other
  10.2 1.3 %wall_round_0.1 = (f32[40,128]{1,0:T(8,128)S(1)}, f32[8,10,128]{2,1,0:T(8,128)S(1)}, f32[12,10,128]{2,1,0:T(8,128)S(1)}, f32[12,10,128]{2,1,0:T(8,128)S(1)}, bf16[25,128,128]{2,1,0:T(8,128)(2,1)S(1)}) custom-call(f32[160,128]{1,0:T(8,128)S(1)} %get-tuple-element.49.own, f32[160,128]{1,0:T(8,128)S(1)} %collective-permute-done.other, bf16[25,128,128]{2,1,0:T(8,128)(2,1)} %bitcast.7), custom_call_target="tpu_custom_call" | custom-call | flops 256000 | bytes 2805760 | tf_op jit(solution)/shard_map/wall_round_0/pallas_call | solution.py:613
  11.5 0.0 collective-permute-done.3.before
  11.5 0.6 %collective-permute-done.2.following = f32[100,128]{1,0:T(8,128)S(1)} collective-permute-done((f32[100,128]{1,0:T(8,128)S(1)}, f32[100,128]{1,0:T(8,128)S(1)}, u32[]{:S(2)}, u32[]{:S(2)}) %collective-permute-start.2) | collective-permute-done | bytes 51232 | tf_op jit(solution)/shard_map/ppermute | solution.py:648
  12.2 0.5 %collective-permute-done.4.refs_1_ = f32[100,128]{1,0:T(8,128)S(1)} collective-permute-done((f32[100,128]{1,0:T(8,128)S(1)}, f32[100,128]{1,0:T(8,128)S(1)}, u32[]{:S(2)}, u32[]{:S(2)}) %collective-permute-start.4) | collective-permute-done | bytes 51232 | tf_op jit(solution)/shard_map/ppermute | solution.py:648
  12.7 0.6 %middle.1 = (f32[40,128]{1,0:T(8,128)S(1)}, f32[6,80,128]{2,1,0:T(8,128)S(1)}, f32[2,40,128]{2,1,0:T(8,128)S(1)}, f32[2,20,128]{2,1,0:T(8,128)S(1)}, f32[2,10,128]{2,1,0:T(8,128)S(1)}) custom-call(f32[100,128]{1,0:T(8,128)S(1)} %get-tuple-element.56.refs_0_, f32[100,128]{1,0:T(8,128)S(1)} %collective-permute-done.4.refs_1_, ...), custom_call_target="tpu_custom_call" | custom-call | flops 8192000 | bytes 4534272 | tf_op jit(solution)/shard_map/middle/pallas_call | solution.py:613
  13.4 2.6 %collective-permute-start.6 = (f32[40,128]{1,0:T(8,128)S(1)}, f32[40,128]{1,0:T(8,128)S(1)}, u32[]{:S(2)}, u32[]{:S(2)}) collective-permute-start(f32[40,128]{1,0:T(8,128)S(1)} %get-tuple-element.78), channel_id=1, source_target_pairs={{0,2},{1,3},{2,1},{3,0},{4,6},{5,7},{6,5},{7,4},{8,10},{9,11},{10,... | collective-permute-start | bytes 61448 | tf_op jit(solution)/shard_map/ppermute | solution.py:648
  16.0 1.2 %collective-permute-start.7 = (f32[40,128]{1,0:T(8,128)S(1)}, f32[40,128]{1,0:T(8,128)S(1)}, u32[]{:S(2)}, u32[]{:S(2)}) collective-permute-start(f32[40,128]{1,0:T(8,128)S(1)} %get-tuple-element.79), channel_id=1, source_target_pairs={{0,3},{1,2},{2,0},{3,1},{4,7},{5,6},{6,4},{7,5},{8,11},{9,10},{10,... | collective-permute-start | bytes 61448 | tf_op jit(solution)/shard_map/ppermute | solution.py:648
  17.2 0.0 collective-permute-start.5
  17.2 1.8 %collective-permute-done.6.refs_5_ = f32[40,128]{1,0:T(8,128)S(1)} collective-permute-done((f32[40,128]{1,0:T(8,128)S(1)}, f32[40,128]{1,0:T(8,128)S(1)}, u32[]{:S(2)}, u32[]{:S(2)}) %collective-permute-start.6) | collective-permute-done | bytes 20512 | tf_op jit(solution)/shard_map/ppermute | solution.py:648
  19.0 1.8 %collective-permute-done.7.refs_6_ = f32[40,128]{1,0:T(8,128)S(1)} collective-permute-done((f32[40,128]{1,0:T(8,128)S(1)}, f32[40,128]{1,0:T(8,128)S(1)}, u32[]{:S(2)}, u32[]{:S(2)}) %collective-permute-start.7) | collective-permute-done | bytes 20512 | tf_op jit(solution)/shard_map/ppermute | solution.py:648
  20.8 0.2 %collective-permute-done.5.refs_4_ = f32[40,128]{1,0:T(8,128)S(1)} collective-permute-done((f32[40,128]{1,0:T(8,128)S(1)}, f32[40,128]{1,0:T(8,128)S(1)}, u32[]{:S(2)}, u32[]{:S(2)}) %collective-permute-start.5) | collective-permute-done | bytes 20512 | tf_op jit(solution)/shard_map/ppermute | solution.py:638
  21.0 0.9 %wall_up.1 = f32[640,128]{1,0:T(8,128)} custom-call(f32[40,128]{1,0:T(8,128)S(1)} %get-tuple-element.50.matrix.refs_0_, f32[12,10,128]{2,1,0:T(8,128)S(1)} %get-tuple-element.51.down_in.refs_1_, f32[12,10,128]{2,1,0:T(8,128)S(1)} %get-tuple-element.52.outer_in.refs_2_, f32[40,128]{1,0:T(8,128)S(1)} %get-tuple-element.77.refs_3_, ...), custom_call_target="tpu_custom_call" | custom-call | flops 2457600 | bytes 2181120 | tf_op jit(solution)/shard_map/wall_up/pallas_call | solution.py:613
  (3 shorter events, 0.1 us)
Async XLA Ops:
  2.2 3.9 %collective-permute-start.1 = (f32[100,128]{1,0:T(8,128)S(1)}, f32[100,128]{1,0:T(8,128)S(1)}, u32[]{:S(2)}, u32[]{:S(2)}) collective-permute-start(f32[100,128]{1,0:T(8,128)S(1)} %get-tuple-element.53.own), channel_id=1, source_target_pairs={{0,4},{4,0},{8,12},{12,8},{16,20},{20,16},{24,28},{28,24},{1,5},{5... | collective-permute-start | bytes 153608 | tf_op jit(solution)/shard_map/ppermute | solution.py:638
  3.5 6.7 %collective-permute-start = (f32[160,128]{1,0:T(8,128)S(1)}, f32[160,128]{1,0:T(8,128)S(1)}, u32[]{:S(2)}, u32[]{:S(2)}) collective-permute-start(f32[160,128]{1,0:T(8,128)S(1)} %get-tuple-element.49.own), channel_id=1, source_target_pairs={{0,1},{1,0},{2,3},{3,2},{4,5},{5,4},{6,7},{7,6},{8,9},{9,8},{10,11... | collective-permute-start | bytes 245768 | tf_op jit(solution)/shard_map/ppermute | solution.py:638
  6.2 5.3 %collective-permute-start.3 = (f32[100,128]{1,0:T(8,128)S(1)}, f32[100,128]{1,0:T(8,128)S(1)}, u32[]{:S(2)}, u32[]{:S(2)}) collective-permute-start(f32[100,128]{1,0:T(8,128)S(1)} %get-tuple-element.55.own), channel_id=1, source_target_pairs={{0,12},{4,8},{8,20},{12,16},{16,28},{20,24},{24,4},{28,0},{1,13},{... | collective-permute-start | bytes 153608 | tf_op jit(solution)/shard_map/ppermute | solution.py:648
  7.5 4.6 %collective-permute-start.2 = (f32[100,128]{1,0:T(8,128)S(1)}, f32[100,128]{1,0:T(8,128)S(1)}, u32[]{:S(2)}, u32[]{:S(2)}) collective-permute-start(f32[100,128]{1,0:T(8,128)S(1)} %get-tuple-element.55.own), channel_id=1, source_target_pairs={{0,28},{4,24},{8,4},{12,0},{16,12},{20,8},{24,20},{28,16},{1,29},{... | collective-permute-start | bytes 153608 | tf_op jit(solution)/shard_map/ppermute | solution.py:648
  8.9 3.8 %collective-permute-start.4 = (f32[100,128]{1,0:T(8,128)S(1)}, f32[100,128]{1,0:T(8,128)S(1)}, u32[]{:S(2)}, u32[]{:S(2)}) collective-permute-start(f32[100,128]{1,0:T(8,128)S(1)} %get-tuple-element.55.own), channel_id=1, source_target_pairs={{0,20},{4,16},{8,28},{12,24},{16,4},{20,0},{24,12},{28,8},{1,21},{... | collective-permute-start | bytes 153608 | tf_op jit(solution)/shard_map/ppermute | solution.py:648
  13.4 5.6 %collective-permute-start.6 = (f32[40,128]{1,0:T(8,128)S(1)}, f32[40,128]{1,0:T(8,128)S(1)}, u32[]{:S(2)}, u32[]{:S(2)}) collective-permute-start(f32[40,128]{1,0:T(8,128)S(1)} %get-tuple-element.78), channel_id=1, source_target_pairs={{0,2},{1,3},{2,1},{3,0},{4,6},{5,7},{6,5},{7,4},{8,10},{9,11},{10,... | collective-permute-start | bytes 61448 | tf_op jit(solution)/shard_map/ppermute | solution.py:648
  16.0 4.8 %collective-permute-start.7 = (f32[40,128]{1,0:T(8,128)S(1)}, f32[40,128]{1,0:T(8,128)S(1)}, u32[]{:S(2)}, u32[]{:S(2)}) collective-permute-start(f32[40,128]{1,0:T(8,128)S(1)} %get-tuple-element.79), channel_id=1, source_target_pairs={{0,3},{1,2},{2,0},{3,1},{4,7},{5,6},{6,4},{7,5},{8,11},{9,10},{10,... | collective-permute-start | bytes 61448 | tf_op jit(solution)/shard_map/ppermute | solution.py:648
  17.2 3.8 %collective-permute-start.5 = (f32[40,128]{1,0:T(8,128)S(1)}, f32[40,128]{1,0:T(8,128)S(1)}, u32[]{:S(2)}, u32[]{:S(2)}) collective-permute-start(f32[40,128]{1,0:T(8,128)S(1)} %get-tuple-element.77.refs_3_), channel_id=1, source_target_pairs={{0,1},{1,0},{2,3},{3,2},{4,5},{5,4},{6,7},{7,6},{8,9},{9,8},{10,11... | collective-permute-start | bytes 61448 | tf_op jit(solution)/shard_map/ppermute | solution.py:638

commit v3 on v2

--- a/solution.py
+++ b/solution.py
@@ -813,8 +813,8 @@
             + [
                 source,
                 exchange(source, "normal", 1 << wall_bits),
-                pass_on(share_two, "normal", wall_bits, (2, 3, 1, 0)),
-                pass_on(share_one, "normal", wall_bits, (3, 2, 0, 1)),
+                pass_on(share_two, "normal", wall_bits, (3, 2, 1, 0)),
+                pass_on(share_one, "normal", wall_bits, (2, 3, 0, 1)),
             ]
             + round_ups
             + round_ws

time: 22 us -> 21.7 us (0.986)
  waiting for transfers between devices: 4.91 us -> 4.01 us
  starting transfers between devices: 11.1 us -> 11.7 us
    ppermute x3, starting transfers between devices: 3.17 us -> 4.89 us  [exchange(): return lax.ppermute(array, axis, [(i, i ^ mask) for i in range(count)])]
    ppermute x5, starting transfers between devices: 7.91 us -> 6.77 us  [pass_on(): return lax.ppermute(array, axis, [(i, target(i)) for i in range(count)])]
    ppermute x5, waiting for transfers between devices: 4.68 us -> 4 us  [pass_on(): return lax.ppermute(array, axis, [(i, target(i)) for i in range(count)])]
    ppermute x3, waiting for transfers between devices: 0.24 us -> 0.01 us  [exchange(): return lax.ppermute(array, axis, [(i, i ^ mask) for i in range(count)])]
  transfers between devices with their start and end apart: 8 -> 8, of which waited for: 5 -> 4; matrix products, arithmetic and copies ran while one was open for 0% -> 0% of each run, Pallas kernels for 10% -> 10%
where the time goes in v3:
time: 21.7 us; the launch traced here: 21.6 us
  starting transfers between devices  11.7 us (54%)
  Pallas kernels  5.83 us (27%)
  waiting for transfers between devices  4.01 us (18%)
    ppermute x5, starting transfers between devices, pass_on(): return lax.ppermute(array, axis, [(i, target(i)) for i in range(count)])  6.77 us
    pallas_call x8, Pallas kernels, kernel(): pl.pallas_call(body, out_shape=[a for a, _ in outs], in_specs=[spec for _...  5.83 us
    ppermute x3, starting transfers between devices, exchange(): return lax.ppermute(array, axis, [(i, i ^ mask) for i in range(count)])  4.89 us
    ppermute x5, waiting for transfers between devices, pass_on(): return lax.ppermute(array, axis, [(i, target(i)) for i in range(count)])  4 us
  transfers between devices with their start and end apart: 8, of which 4 were waited for; matrix products, arithmetic and copies ran while one was open for 0% of the time, Pallas kernels for 10%

profile of v3, /device:TPU:0, one launch (start us, length us, event | category | flops | bytes accessed | tf_op | source)
XLA Modules:
  0.0 21.6 jit_solution(16266345172582101154)
XLA Ops:
  0.0 2.2 %wrap_down.1 = (f32[100,128]{1,0:T(8,128)S(1)}, f32[56,40,128]{2,1,0:T(8,128)S(1)}, f32[14,40,128]{2,1,0:T(8,128)S(1)}, f32[8,20,128]{2,1,0:T(8,128)S(1)}, f32[8...) custom-call(f32[640,128]{1,0:T(8,128)} %bitcast.8, ...), custom_call_target="tpu_custom_call" | custom-call | flops 8192000 | bytes 3171328 | tf_op jit(solution)/shard_map/wrap_down/pallas_call | solution.py:613
  2.2 0.5 %collective-permute-start.1 = (f32[100,128]{1,0:T(8,128)S(1)}, f32[100,128]{1,0:T(8,128)S(1)}, u32[]{:S(2)}, u32[]{:S(2)}) collective-permute-start(f32[100,128]{1,0:T(8,128)S(1)} %get-tuple-element.53.own), channel_id=1, source_target_pairs={{0,4},{4,0},{8,12},{12,8},{16,20},{20,16},{24,28},{28,24},{1,5},{5... | collective-permute-start | bytes 153608 | tf_op jit(solution)/shard_map/ppermute | solution.py:638
  2.7 0.7 %wall_matrix.1 = (f32[160,128]{1,0:T(8,128)S(1)}, f32[6,16,128]{2,1,0:T(8,128)S(1)}, f32[24,80,128]{2,1,0:T(8,128)S(1)}, f32[27,80,128]{2,1,0:T(8,128)S(1)}, f32...) custom-call(f32[640,128]{1,0:T(8,128)S(1)} %get-tuple-element.47.ref, ...), custom_call_target="tpu_custom_call" | custom-call | flops 8192000 | bytes 3330048 | tf_op jit(solution)/shard_map/wall_matrix/pallas_call | solution.py:613
  3.5 2.7 %collective-permute-start = (f32[160,128]{1,0:T(8,128)S(1)}, f32[160,128]{1,0:T(8,128)S(1)}, u32[]{:S(2)}, u32[]{:S(2)}) collective-permute-start(f32[160,128]{1,0:T(8,128)S(1)} %get-tuple-element.49.own), channel_id=1, source_target_pairs={{0,1},{1,0},{2,3},{3,2},{4,5},{5,4},{6,7},{7,6},{8,9},{9,8},{10,11... | collective-permute-start | bytes 245768 | tf_op jit(solution)/shard_map/ppermute | solution.py:638
  6.1 0.0 collective-permute-done.1.other
  6.2 1.4 %collective-permute-start.3 = (f32[100,128]{1,0:T(8,128)S(1)}, f32[100,128]{1,0:T(8,128)S(1)}, u32[]{:S(2)}, u32[]{:S(2)}) collective-permute-start(f32[100,128]{1,0:T(8,128)S(1)} %get-tuple-element.55.own), channel_id=1, source_target_pairs={{0,12},{4,8},{8,20},{12,16},{16,28},{20,24},{24,4},{28,0},{1,13},{... | collective-permute-start | bytes 153608 | tf_op jit(solution)/shard_map/ppermute | solution.py:648
  7.5 1.3 %collective-permute-start.2 = (f32[100,128]{1,0:T(8,128)S(1)}, f32[100,128]{1,0:T(8,128)S(1)}, u32[]{:S(2)}, u32[]{:S(2)}) collective-permute-start(f32[100,128]{1,0:T(8,128)S(1)} %get-tuple-element.55.own), channel_id=1, source_target_pairs={{0,28},{4,24},{8,4},{12,0},{16,12},{20,8},{24,20},{28,16},{1,29},{... | collective-permute-start | bytes 153608 | tf_op jit(solution)/shard_map/ppermute | solution.py:648
  8.9 1.3 %collective-permute-start.4 = (f32[100,128]{1,0:T(8,128)S(1)}, f32[100,128]{1,0:T(8,128)S(1)}, u32[]{:S(2)}, u32[]{:S(2)}) collective-permute-start(f32[100,128]{1,0:T(8,128)S(1)} %get-tuple-element.55.own), channel_id=1, source_target_pairs={{0,20},{4,16},{8,28},{12,24},{16,4},{20,0},{24,12},{28,8},{1,21},{... | collective-permute-start | bytes 153608 | tf_op jit(solution)/shard_map/ppermute | solution.py:648
  10.2 0.0 collective-permute-done.other
  10.2 1.3 %wall_round_0.1 = (f32[40,128]{1,0:T(8,128)S(1)}, f32[8,10,128]{2,1,0:T(8,128)S(1)}, f32[12,10,128]{2,1,0:T(8,128)S(1)}, f32[12,10,128]{2,1,0:T(8,128)S(1)}, bf16[25,128,128]{2,1,0:T(8,128)(2,1)S(1)}) custom-call(f32[160,128]{1,0:T(8,128)S(1)} %get-tuple-element.49.own, f32[160,128]{1,0:T(8,128)S(1)} %collective-permute-done.other, bf16[25,128,128]{2,1,0:T(8,128)(2,1)} %bitcast.7), custom_call_target="tpu_custom_call" | custom-call | flops 256000 | bytes 2805760 | tf_op jit(solution)/shard_map/wall_round_0/pallas_call | solution.py:613
  11.5 0.0 collective-permute-done.3.before
  11.5 0.6 %collective-permute-done.2.following = f32[100,128]{1,0:T(8,128)S(1)} collective-permute-done((f32[100,128]{1,0:T(8,128)S(1)}, f32[100,128]{1,0:T(8,128)S(1)}, u32[]{:S(2)}, u32[]{:S(2)}) %collective-permute-start.2) | collective-permute-done | bytes 51232 | tf_op jit(solution)/shard_map/ppermute | solution.py:648
  12.2 0.5 %collective-permute-done.4.refs_1_ = f32[100,128]{1,0:T(8,128)S(1)} collective-permute-done((f32[100,128]{1,0:T(8,128)S(1)}, f32[100,128]{1,0:T(8,128)S(1)}, u32[]{:S(2)}, u32[]{:S(2)}) %collective-permute-start.4) | collective-permute-done | bytes 51232 | tf_op jit(solution)/shard_map/ppermute | solution.py:648
  12.7 0.6 %middle.1 = (f32[40,128]{1,0:T(8,128)S(1)}, f32[6,80,128]{2,1,0:T(8,128)S(1)}, f32[2,40,128]{2,1,0:T(8,128)S(1)}, f32[2,20,128]{2,1,0:T(8,128)S(1)}, f32[2,10,128]{2,1,0:T(8,128)S(1)}) custom-call(f32[100,128]{1,0:T(8,128)S(1)} %get-tuple-element.56.refs_0_, f32[100,128]{1,0:T(8,128)S(1)} %collective-permute-done.4.refs_1_, ...), custom_call_target="tpu_custom_call" | custom-call | flops 8192000 | bytes 4534272 | tf_op jit(solution)/shard_map/middle/pallas_call | solution.py:613
  13.4 2.5 %collective-permute-start.6 = (f32[40,128]{1,0:T(8,128)S(1)}, f32[40,128]{1,0:T(8,128)S(1)}, u32[]{:S(2)}, u32[]{:S(2)}) collective-permute-start(f32[40,128]{1,0:T(8,128)S(1)} %get-tuple-element.78), channel_id=1, source_target_pairs={{0,3},{1,2},{2,1},{3,0},{4,7},{5,6},{6,5},{7,4},{8,11},{9,10},{10,... | collective-permute-start | bytes 61448 | tf_op jit(solution)/shard_map/ppermute | solution.py:648
  15.9 0.2 collective-permute-start.7
  16.1 1.7 %collective-permute-start.5 = (f32[40,128]{1,0:T(8,128)S(1)}, f32[40,128]{1,0:T(8,128)S(1)}, u32[]{:S(2)}, u32[]{:S(2)}) collective-permute-start(f32[40,128]{1,0:T(8,128)S(1)} %get-tuple-element.77.refs_3_), channel_id=1, source_target_pairs={{0,1},{1,0},{2,3},{3,2},{4,5},{5,4},{6,7},{7,6},{8,9},{9,8},{10,11... | collective-permute-start | bytes 61448 | tf_op jit(solution)/shard_map/ppermute | solution.py:638
  17.8 1.2 %collective-permute-done.6.refs_5_ = f32[40,128]{1,0:T(8,128)S(1)} collective-permute-done((f32[40,128]{1,0:T(8,128)S(1)}, f32[40,128]{1,0:T(8,128)S(1)}, u32[]{:S(2)}, u32[]{:S(2)}) %collective-permute-start.6) | collective-permute-done | bytes 20512 | tf_op jit(solution)/shard_map/ppermute | solution.py:648
  19.0 1.7 %collective-permute-done.7.refs_6_ = f32[40,128]{1,0:T(8,128)S(1)} collective-permute-done((f32[40,128]{1,0:T(8,128)S(1)}, f32[40,128]{1,0:T(8,128)S(1)}, u32[]{:S(2)}, u32[]{:S(2)}) %collective-permute-start.7) | collective-permute-done | bytes 20512 | tf_op jit(solution)/shard_map/ppermute | solution.py:648
  20.7 0.0 collective-permute-done.5.refs_4_
  20.7 0.9 %wall_up.1 = f32[640,128]{1,0:T(8,128)} custom-call(f32[40,128]{1,0:T(8,128)S(1)} %get-tuple-element.50.matrix.refs_0_, f32[12,10,128]{2,1,0:T(8,128)S(1)} %get-tuple-element.51.down_in.refs_1_, f32[12,10,128]{2,1,0:T(8,128)S(1)} %get-tuple-element.52.outer_in.refs_2_, f32[40,128]{1,0:T(8,128)S(1)} %get-tuple-element.77.refs_3_, ...), custom_call_target="tpu_custom_call" | custom-call | flops 2457600 | bytes 2181120 | tf_op jit(solution)/shard_map/wall_up/pallas_call | solution.py:613
  (3 shorter events, 0.1 us)
Async XLA Ops:
  2.2 3.9 %collective-permute-start.1 = (f32[100,128]{1,0:T(8,128)S(1)}, f32[100,128]{1,0:T(8,128)S(1)}, u32[]{:S(2)}, u32[]{:S(2)}) collective-permute-start(f32[100,128]{1,0:T(8,128)S(1)} %get-tuple-element.53.own), channel_id=1, source_target_pairs={{0,4},{4,0},{8,12},{12,8},{16,20},{20,16},{24,28},{28,24},{1,5},{5... | collective-permute-start | bytes 153608 | tf_op jit(solution)/shard_map/ppermute | solution.py:638
  3.5 6.7 %collective-permute-start = (f32[160,128]{1,0:T(8,128)S(1)}, f32[160,128]{1,0:T(8,128)S(1)}, u32[]{:S(2)}, u32[]{:S(2)}) collective-permute-start(f32[160,128]{1,0:T(8,128)S(1)} %get-tuple-element.49.own), channel_id=1, source_target_pairs={{0,1},{1,0},{2,3},{3,2},{4,5},{5,4},{6,7},{7,6},{8,9},{9,8},{10,11... | collective-permute-start | bytes 245768 | tf_op jit(solution)/shard_map/ppermute | solution.py:638
  6.2 5.3 %collective-permute-start.3 = (f32[100,128]{1,0:T(8,128)S(1)}, f32[100,128]{1,0:T(8,128)S(1)}, u32[]{:S(2)}, u32[]{:S(2)}) collective-permute-start(f32[100,128]{1,0:T(8,128)S(1)} %get-tuple-element.55.own), channel_id=1, source_target_pairs={{0,12},{4,8},{8,20},{12,16},{16,28},{20,24},{24,4},{28,0},{1,13},{... | collective-permute-start | bytes 153608 | tf_op jit(solution)/shard_map/ppermute | solution.py:648
  7.5 4.6 %collective-permute-start.2 = (f32[100,128]{1,0:T(8,128)S(1)}, f32[100,128]{1,0:T(8,128)S(1)}, u32[]{:S(2)}, u32[]{:S(2)}) collective-permute-start(f32[100,128]{1,0:T(8,128)S(1)} %get-tuple-element.55.own), channel_id=1, source_target_pairs={{0,28},{4,24},{8,4},{12,0},{16,12},{20,8},{24,20},{28,16},{1,29},{... | collective-permute-start | bytes 153608 | tf_op jit(solution)/shard_map/ppermute | solution.py:648
  8.9 3.8 %collective-permute-start.4 = (f32[100,128]{1,0:T(8,128)S(1)}, f32[100,128]{1,0:T(8,128)S(1)}, u32[]{:S(2)}, u32[]{:S(2)}) collective-permute-start(f32[100,128]{1,0:T(8,128)S(1)} %get-tuple-element.55.own), channel_id=1, source_target_pairs={{0,20},{4,16},{8,28},{12,24},{16,4},{20,0},{24,12},{28,8},{1,21},{... | collective-permute-start | bytes 153608 | tf_op jit(solution)/shard_map/ppermute | solution.py:648
  13.4 5.6 %collective-permute-start.6 = (f32[40,128]{1,0:T(8,128)S(1)}, f32[40,128]{1,0:T(8,128)S(1)}, u32[]{:S(2)}, u32[]{:S(2)}) collective-permute-start(f32[40,128]{1,0:T(8,128)S(1)} %get-tuple-element.78), channel_id=1, source_target_pairs={{0,3},{1,2},{2,1},{3,0},{4,7},{5,6},{6,5},{7,4},{8,11},{9,10},{10,... | collective-permute-start | bytes 61448 | tf_op jit(solution)/shard_map/ppermute | solution.py:648
  15.9 4.8 %collective-permute-start.7 = (f32[40,128]{1,0:T(8,128)S(1)}, f32[40,128]{1,0:T(8,128)S(1)}, u32[]{:S(2)}, u32[]{:S(2)}) collective-permute-start(f32[40,128]{1,0:T(8,128)S(1)} %get-tuple-element.79), channel_id=1, source_target_pairs={{0,2},{1,3},{2,0},{3,1},{4,6},{5,7},{6,4},{7,5},{8,10},{9,11},{10,... | collective-permute-start | bytes 61448 | tf_op jit(solution)/shard_map/ppermute | solution.py:648
  16.1 4.6 %collective-permute-start.5 = (f32[40,128]{1,0:T(8,128)S(1)}, f32[40,128]{1,0:T(8,128)S(1)}, u32[]{:S(2)}, u32[]{:S(2)}) collective-permute-start(f32[40,128]{1,0:T(8,128)S(1)} %get-tuple-element.77.refs_3_), channel_id=1, source_target_pairs={{0,1},{1,0},{2,3},{3,2},{4,5},{5,4},{6,7},{7,6},{8,9},{9,8},{10,11... | collective-permute-start | bytes 61448 | tf_op jit(solution)/shard_map/ppermute | solution.py:638
